TPU v7x, 256 devices: a whole 4x4x8 slice. The times are simulated.
256 devices in a mesh: tower: 2 (over x_lo), dp: 32 (over x_hi, z, core), mp: 4 (over y).
Axes of the slice: x: 4 (x_hi: 2, x_lo: 2; x = x_hi * 2 + x_lo), y: 4, z: 8, core: 2. Of those that a mesh axis runs over, the one named last changes fastest.
Arguments:
- inputs: bfloat16 [2, 16384, 1792], P('tower', 'dp', 'mp'), may hold values from -6 to 6
- weights: bfloat16 [2, 1792, 1152], P('tower', 'mp'), may hold values from -0.125 to 0.125
- pair_ids: int32 [16384], P('dp'), may hold values from 0 to 32767
Outputs:
- row_loss: float32 [2, 16384], P('tower', 'dp')
- input_grad: bfloat16 [2, 16384, 1792], P('tower', 'dp', 'mp')
- weight_grad: float32 [2, 1792, 1152], P('tower', ('mp', 'dp'))
Inputs may be any that keep to these rules, and one draw needn't show every extreme that they name: `pair_ids`: row i's image and text form pair i; rows with equal ids are positive pairs, all others negative.
All inputs are finite; a program needn't handle non-finite values.
Results may differ from a plain program's by a relative error of at most 0.015.
Values may be sent and summed in bfloat16 or wider, within the bound.
A program may use at most 64 MiB of HBM per device.

v0:
```python
import jax
import jax.numpy as jnp
from jax import lax
from jax.sharding import PartitionSpec as P

logit_scale = 100.0
pair_logit_bias = -6.0
norm_eps = 1e-06


def partner_2(array, axis, stride):
    return lax.ppermute(array, axis, [(i, i ^ 1 << stride) for i in range(lax.axis_size(axis))])


def pair_terms(local_unit_rows, own_ids, partner_unit_rows, other_ids):
    pair_logits = (
        logit_scale
        * jnp.dot(local_unit_rows, partner_unit_rows.T, preferred_element_type=jnp.float32)
        + pair_logit_bias
    )
    label_sign = jnp.where(own_ids[:, None] == other_ids[None, :], 1.0, -1.0).astype(jnp.float32)
    pair_loss = jax.nn.softplus(-label_sign * pair_logits)
    slope_bias_gradient = (-label_sign * jax.nn.sigmoid(-label_sign * pair_logits)).astype(
        jnp.bfloat16
    )
    return (pair_loss, slope_bias_gradient)


def local(inputs, weights, pair_ids):
    own_rows = inputs[0]
    local_weight = weights[0]
    row_count = own_rows.shape[0]
    quarter = row_count // lax.axis_size("mp")
    row_start = lax.axis_index("mp") * quarter
    partial_value = jnp.dot(own_rows, local_weight, preferred_element_type=jnp.float32)
    embedding = lax.psum(partial_value, "mp")
    inverse_norm = lax.rsqrt(jnp.sum(embedding * embedding, axis=1, keepdims=True) + norm_eps)
    unit_vec = embedding * inverse_norm
    unit_b = unit_vec.astype(jnp.bfloat16)
    mine = lax.dynamic_slice_in_dim(unit_b, row_start, quarter, 0)
    mine_ids = lax.dynamic_slice_in_dim(pair_ids, row_start, quarter, 0)
    partner = partner_2(mine, "tower", 0)
    partner_block = lax.all_gather(partner, "dp", axis=0, tiled=True)
    other_ids = lax.all_gather(mine_ids, "dp", axis=0, tiled=True)
    pair_loss, slope_bias_gradient = pair_terms(unit_b, pair_ids, partner_block, other_ids)
    local_gradient = logit_scale * jnp.dot(
        slope_bias_gradient, partner_block, preferred_element_type=jnp.float32
    )
    local_gradient, loss_own = (local_gradient, jnp.sum(pair_loss, axis=1))
    unit_grad, loss_total = lax.psum((local_gradient, loss_own), "mp")
    inner = jnp.sum(unit_vec * unit_grad, axis=1, keepdims=True)
    delta_b = ((unit_grad - unit_vec * inner) * inverse_norm).astype(jnp.bfloat16)
    feature_grad = jnp.dot(delta_b, local_weight.T, preferred_element_type=jnp.float32).astype(
        jnp.bfloat16
    )
    matrix_grad = lax.psum_scatter(
        jnp.dot(own_rows.T, delta_b, preferred_element_type=jnp.float32).astype(jnp.bfloat16),
        "dp",
        scatter_dimension=0,
        tiled=True,
    ).astype(jnp.float32)
    batch_total = row_count * lax.axis_size("dp")
    row_loss = loss_total / batch_total
    return (row_loss[None], feature_grad[None], matrix_grad[None])


def solution(mesh):
    placed = (P("tower", "dp", "mp"), P("tower", "mp", None), P("dp"))
    return jax.shard_map(
        local,
        mesh=mesh,
        in_specs=placed,
        out_specs=(P("tower", "dp"), P("tower", "dp", "mp"), P("tower", ("mp", "dp"), None)),
        check_vma=False,
    )
```

profile of v0, /device:TPU:6, one launch (start us, length us, event | category | flops | bytes accessed | tf_op | source)
XLA Modules:
  0.0 392.1 jit_solution(13105302145818052880)
XLA Ops:
  7.2 0.0 copy-start
  7.2 0.0 all-reduce.5.cloned.1.call-start
  7.2 1.2 copy-done
  8.4 3.3 fusion.7
  11.7 0.0 all-reduce.5.cloned.1.call-update
  11.7 0.0 all-gather.3.cloned.1.call-start
  11.8 71.1 %all-reduce.5.cloned.1.call-done = f32[512,1152]{1,0:T(8,128)} async-done(((f32[512,1152]{1,0:T(8,128)}), f32[512,1152]{1,0:T(8,128)}) %all-reduce.5.cloned.1.call-update) | async-done | bytes 2359312 | tf_op jit(solution)/shard_map/psum | solution.py:36
  82.9 2.0 multiply_reduce_fusion.1
  84.9 0.3 copy-done.1
  85.3 0.2 multiply_convert_fusion.5
  85.5 0.0 copy-start.3
  85.5 1.0 copy-done.3
  86.5 0.9 collective-permute-start
  87.4 8.0 %collective-permute-done = bf16[128,1152]{1,0:T(8,128)(2,1)} collective-permute-done((bf16[128,1152]{1,0:T(8,128)(2,1)S(1)}, bf16[128,1152]{1,0:T(8,128)(2,1)}, u32[]{:S(2)}, u32[]{:S(2)}) %collective-permute-start) | collective-permute-done | bytes 294944 | tf_op jit(solution)/shard_map/ppermute | solution.py:12
  95.4 0.0 all-gather.3.cloned.1.call-update
  95.4 0.0 all-reduce.7.cloned.1.call-start
  95.5 0.0 copy-done.8
  95.5 0.1 dynamic-slice_bitcast_fusion.1
  95.6 40.4 %all-gather = s32[32,1,128]{2,1,0:T(1,128)S(1)} all-gather(s32[1,1,128]{2,1,0:T(1,128)S(1)} %dynamic-slice_bitcast_fusion.1), channel_id=1, replica_groups=mesh['tower'=2,'dp'=32,'mp'=4] {'dp'}, dimensions={0}, use_global_device_ids=true | all-gather | bytes 16896 | tf_op jit(solution)/shard_map/all_gather | solution.py:44
  135.9 63.3 %all-gather.3.cloned.1.call-done = bf16[4096,1152]{1,0:T(8,128)(2,1)} async-done(((bf16[128,1152]{1,0:T(8,128)(2,1)}), bf16[4096,1152]{1,0:T(8,128)(2,1)}) %all-gather.3.cloned.1.call-update) | async-done | bytes 9437200 | tf_op jit(solution)/shard_map/all_gather | solution.py:43
  199.3 12.5 %fusion.1 = (f32[512]{0:T(512)S(1)}, f32[512,4096]{1,0:T(8,128)S(1)}) fusion(bf16[512,1152]{1,0:T(8,128)(2,1)} %copy-done.3, bf16[4096,1152]{1,0:T(8,128)(2,1)} %all-gather.3.cloned.1.call-done, s32[4096]{0:T(1024)S(1)} %bitcast.31, s32[512]{0:T(512)S(1)} %copy-done.8), kind=kOutput, calls=%fused_computation.1 | convolution fusion | flops 4859100672 | bytes 19025920 | tf_op jit(solution)/shard_map/dot_general | solution.py:18
  211.8 0.0 copy-done.7
  211.8 8.3 %fusion.3 = f32[512,1152]{1,0:T(8,128)} fusion(bf16[4096,1152]{1,0:T(8,128)(2,1)S(1)} %copy-done.7, f32[512,4096]{1,0:T(8,128)S(1)} %get-tuple-element.10, s32[4096]{0:T(1024)S(1)} %bitcast.32, s32[512]{0:T(512)S(1)} %copy-done.8), kind=kOutput, calls=%fused_computation.6 | convolution fusion | flops 4849205248 | bytes 20203520 | tf_op jit(solution)/shard_map/dot_general | solution.py:46
  220.1 0.0 all-reduce.7.cloned.1.call-update
  220.1 0.7 copy-done.6
  220.8 0.6 dynamic-slice.4
  222.0 10.5 %psum.22 = f32[512]{0:T(512)S(1)} all-reduce(f32[512]{0:T(512)S(1)} %get-tuple-element.9), channel_id=1, replica_groups=mesh['tower'=2,'dp'=32,'mp'=4] {'mp'}, use_global_device_ids=true, to_apply=%region_3.4 | all-reduce | flops 512 | bytes 4096 | tf_op jit(solution)/shard_map/psum | solution.py:50
  232.5 0.6 broadcast_multiply_fusion
  233.1 53.3 %all-reduce.7.cloned.1.call-done = f32[512,1152]{1,0:T(8,128)} async-done(((f32[512,1152]{1,0:T(8,128)}), f32[512,1152]{1,0:T(8,128)}) %all-reduce.7.cloned.1.call-update) | async-done | bytes 2359312 | tf_op jit(solution)/shard_map/psum | solution.py:50
  286.4 2.2 multiply_reduce_fusion
  288.6 0.2 copy-done.2
  288.8 0.4 multiply_convert_fusion.4
  289.3 0.0 copy-start.4
  289.3 1.0 copy-done.4
  290.3 0.0 copy-done.5
  290.3 0.8 fusion.4
  291.0 76.1 %fusion = bf16[16,1152]{1,0:T(8,128)(2,1)S(1)} fusion(bf16[448,1152]{1,0:T(8,128)(2,1)S(1)} %fusion.4), kind=kCustom, calls=%all-reduce-scatter | all-reduce-scatter fusion | flops 589825 | bytes 1070080
  367.2 1.9 collective-permute-start.3
  369.1 1.9 collective-permute-start.2
  371.1 1.9 collective-permute-start.1
  373.0 1.9 collective-permute-start.4
  374.9 2.8 fusion.5
  377.7 6.4 %collective-permute-done.4 = bf16[14,1152]{1,0:T(8,128)(2,1)S(1)} collective-permute-done((bf16[14,1152]{1,0:T(8,128)(2,1)S(1)}, bf16[14,1152]{1,0:T(8,128)(2,1)S(1)}, u32[]{:S(2)}, u32[]{:S(2)}) %collective-permute-start.4) | collective-permute-done | bytes 32288
  384.1 0.0 collective-permute-done.3
  384.1 0.0 collective-permute-done.2
  384.1 0.0 collective-permute-done.1
  384.1 0.8 concatenate
  384.9 0.7 copy.7
  (10 shorter events, 0.1 us)
Async XLA Ops:
  7.2 1.2 copy-start
  7.2 75.7 %all-reduce.5.cloned.1.call-start = ((), (), s32[]{:S(2)}) async-start(), calls=%async_computation | async-start | bytes 4718592 | tf_op jit(solution)/shard_map/psum | solution.py:36
  11.7 187.6 %all-gather.3.cloned.1.call-start = ((), (), s32[]{:S(2)}) async-start(), calls=%async_computation.1 | async-start | bytes 9732096 | tf_op jit(solution)/shard_map/all_gather | solution.py:43
  82.9 2.4 copy-start.1
  84.9 10.6 %copy-start.8 = (s32[512]{0:T(512)S(1)}, s32[512]{0:T(512)}, u32[]{:S(2)}) copy-start(s32[512]{0:T(512)} %param.5) | copy-start | bytes 6148
  85.5 1.0 copy-start.3
  86.5 8.9 %collective-permute-start = (bf16[128,1152]{1,0:T(8,128)(2,1)S(1)}, bf16[128,1152]{1,0:T(8,128)(2,1)}, u32[]{:S(2)}, u32[]{:S(2)}) collective-permute-start(bf16[128,1152]{1,0:T(8,128)(2,1)S(1)} %constant_dynamic-slice_fusion), channel_id=1, source_target_pairs={{0,128},{128,0},{1,129},{129,1},{2,130},{130,2},{3,131},{131,3},{4... | collective-permute-start | bytes 884744 | tf_op jit(solution)/shard_map/ppermute | solution.py:12
  95.4 191.0 %all-reduce.7.cloned.1.call-start = ((), (), s32[]{:S(2)}) async-start(), calls=%async_computation.2 | async-start | bytes 4718592 | tf_op jit(solution)/shard_map/psum | solution.py:50
  199.3 12.6 %copy-start.7 = (bf16[4096,1152]{1,0:T(8,128)(2,1)S(1)}, bf16[4096,1152]{1,0:T(8,128)(2,1)}, u32[]{:S(2)}) copy-start(bf16[4096,1152]{1,0:T(8,128)(2,1)} %all-gather.3.cloned.1.call-done) | copy-start | bytes 28311556
  220.1 0.7 copy-start.6
  286.4 2.4 copy-start.2
  288.8 1.5 copy-start.5
  289.3 1.0 copy-start.4
  367.2 16.9 %collective-permute-start.3 = (bf16[16,1152]{1,0:T(8,128)(2,1)S(1)}, bf16[16,1152]{1,0:T(8,128)(2,1)S(1)}, u32[]{:S(2)}, u32[]{:S(2)}) collective-permute-start(bf16[16,1152]{1,0:T(8,128)(2,1)S(1)} %fusion), channel_id=1, source_target_pairs={{0,12},{4,16},{8,20},{12,24},{16,28},{20,32},{24,36},{28,40},{32,4... | collective-permute-start | bytes 110600
  369.1 15.0 %collective-permute-start.2 = (bf16[16,1152]{1,0:T(8,128)(2,1)S(1)}, bf16[16,1152]{1,0:T(8,128)(2,1)S(1)}, u32[]{:S(2)}, u32[]{:S(2)}) collective-permute-start(bf16[16,1152]{1,0:T(8,128)(2,1)S(1)} %fusion), channel_id=1, source_target_pairs={{0,8},{4,12},{8,16},{12,20},{16,24},{20,28},{24,32},{28,36},{32,40... | collective-permute-start | bytes 110600
  371.1 13.1 %collective-permute-start.1 = (bf16[16,1152]{1,0:T(8,128)(2,1)S(1)}, bf16[16,1152]{1,0:T(8,128)(2,1)S(1)}, u32[]{:S(2)}, u32[]{:S(2)}) collective-permute-start(bf16[16,1152]{1,0:T(8,128)(2,1)S(1)} %fusion), channel_id=1, source_target_pairs={{0,4},{4,8},{8,12},{12,16},{16,20},{20,24},{24,28},{28,32},{32,36}... | collective-permute-start | bytes 110600
  373.0 11.1 %collective-permute-start.4 = (bf16[14,1152]{1,0:T(8,128)(2,1)S(1)}, bf16[14,1152]{1,0:T(8,128)(2,1)S(1)}, u32[]{:S(2)}, u32[]{:S(2)}) collective-permute-start(bf16[14,1152]{1,0:T(8,128)(2,1)S(1)} %slice), channel_id=1, source_target_pairs={{0,16},{4,20},{8,24},{12,28},{16,32},{20,36},{24,40},{28,44},{32,4... | collective-permute-start | bytes 96776
Sparse Core Ops, SparseCore 0:
  11.8 71.0 all-reduce.4
  95.6 103.6 all-gather.2
  220.2 66.1 all-reduce.6
where the time goes:
time: 393 us; the launch traced here: 392 us
  waiting for transfers between devices  202 us (51%)
  blocking collectives  127 us (32%)
  matrix products  27.7 us (7%)
  between operations  14.6 us (4%)
  starting transfers between devices  8.74 us (2%)
  local copies, waits for them, and re-layouts  6.49 us (2%)
  other arithmetic  5.48 us (1%)
    unnamed x1, blocking collectives  76.1 us
    psum x1, waiting for transfers between devices, local(): embedding = lax.psum(partial_value, 'mp')  71.1 us
    all_gather x1, waiting for transfers between devices, local(): partner_block = lax.all_gather(partner, 'dp', axis=0, tiled=True)  63.3 us
    psum x1, waiting for transfers between devices, local(): unit_grad, loss_total = lax.psum((local_gradient, loss_own), 'mp')  53.3 us
    all_gather x1, blocking collectives, local(): other_ids = lax.all_gather(mine_ids, 'dp', axis=0, tiled=True)  40.4 us
    dot_general x1, matrix products, pair_terms(): jnp.dot(local_unit_rows, partner_unit_rows.T, preferred_element_type=jnp....  12.5 us
    psum x1, blocking collectives, local(): unit_grad, loss_total = lax.psum((local_gradient, loss_own), 'mp')  10.5 us
    dot_general x1, matrix products, local(): jnp.dot(slope_bias_gradient, partner_block, preferred_element_type=jnp.fl...  8.25 us
  transfers between devices with their start and end apart: 8, of which 5 were waited for; matrix products, arithmetic and copies ran while one was open for 1% of the time, Pallas kernels for 0%

commit v1 on v0

v1 whole, which is shorter than its diff:
```python
import functools

import jax
import jax.numpy as jnp
from jax import lax
from jax.experimental import pallas as pl
from jax.experimental.pallas import tpu as pltpu
from jax.sharding import PartitionSpec as P

MESH = pl.DeviceIdType.MESH
F32, BF16, I32 = jnp.float32, jnp.bfloat16, jnp.int32
LOGIT_SCALE = 100.0
LOGIT_BIAS = -6.0
NORM_EPS = 1e-06
LOG2E = 1.4426950408889634
LN2 = 0.6931471805599453

E = 1152
Q = 128
H = 64
NT = (((1,), (1,)), ((), ()))


def kernel(x, w, ids, loss_out, dx_out, dw_out, *scratch):
    (
        unit, unit_own, inv_own, part_f, part_own,
        e_send, e_opp, e_recv,
        cols, ring, col_ids, row_ids, sel, xpad, logits, slope, acc, lacc,
        g_send, g_opp, g_recv,
        loss_v, delta, dw_acc, sib_dw, zs_send, zs_recv, x_recv, x_send,
        s_e, r_e, s_i, r_i, s_u, r_u, s_x1, r_x1, s_z1, r_z1, s_z2, r_z2, s_x2, r_x2,
        s_sib, r_sib, s_g, r_g, s_l, r_l, s_d, r_d, s_w, r_w,
    ) = scratch
    t, d, m = lax.axis_index("tower"), lax.axis_index("dp"), lax.axis_index("mp")
    c, z, xh = lax.rem(d, 2), lax.rem(d // 2, 8), d // 16

    def at_dp(xh_, z_, c_):
        return (xh_ * 8 + z_) * 2 + c_

    def zoff(k):
        return lax.rem(z + (k + 8), 8)

    def moff(k):
        return lax.rem(m + (k + 4), 4)

    x_same, x_other = (1 - t, d, m), (1 - t, at_dp(1 - xh, z, c), m)
    z_dev = ((t, at_dp(xh, zoff(1), c), m), (t, at_dp(xh, zoff(-1), c), m))
    y_dev = ((t, d, moff(1)), (t, d, moff(-1)))
    sibling = (t, at_dp(xh, z, 1 - c), m)
    x_far = (t, at_dp(1 - xh, z, c), m)
    others = (x_same, x_other, *z_dev, *y_dev, sibling, x_far)

    sends = []

    def send(src, dst, ss, rs, dev):
        copy = pltpu.make_async_remote_copy(
            src_ref=src, dst_ref=dst, send_sem=ss, recv_sem=rs, device_id=dev, device_id_type=MESH
        )
        copy.start()
        sends.append(copy)

    def recv(dst, rs):
        pltpu.make_async_remote_copy(
            src_ref=dst, dst_ref=dst, send_sem=rs, recv_sem=rs, device_id=sibling, device_id_type=MESH
        ).wait_recv()

    def rows_of(q, lo=0, n=Q):
        return pl.ds(pl.multiple_of(q * Q + lo, 16), n)

    q_opp, q_p, q_m = moff(2), moff(1), moff(-1)
    lo_h, hi_h = pl.ds(0, H), pl.ds(H, H)

    barrier = pltpu.get_barrier_semaphore()
    for dev in others:
        pl.semaphore_signal(barrier, inc=1, device_id=dev, device_id_type=MESH)

    def project(q):
        return jnp.dot(x[rows_of(q), :], w[...], preferred_element_type=F32)

    e_send[0] = project(q_opp).astype(BF16)
    pl.semaphore_wait(barrier, len(others))

    def exchange_opposite(buf, opp, ss, rs):
        send(buf.at[0, lo_h], opp.at[0], ss.at[0], rs.at[0], y_dev[0])
        send(buf.at[0, hi_h], opp.at[1], ss.at[1], rs.at[1], y_dev[1])

    def exchange_direct(k, buf, got, ss, rs):
        half = hi_h if k == 0 else lo_h
        send(buf.at[1 + k, half], got.at[k, half], ss.at[2 + k], rs.at[2 + k], y_dev[k])

    def exchange_sum(k, buf, opp, got, ss, rs, own):
        half = lo_h if k == 0 else hi_h
        recv(opp.at[k], rs.at[k])
        buf[1 + k, half, :] = (own + opp[k].astype(F32)).astype(BF16)
        send(buf.at[1 + k, half], got.at[k, half], ss.at[4 + k], rs.at[4 + k], y_dev[k])

    def exchange_total(got, rs, own):
        for k in range(2):
            recv(got.at[k, hi_h if k == 0 else lo_h], rs.at[2 + k])
            recv(got.at[k, lo_h if k == 0 else hi_h], rs.at[4 + k])
        return own + got[0].astype(F32) + got[1].astype(F32)

    exchange_opposite(e_send, e_opp, s_e, r_e)
    col_ids[z, pl.ds(xh * 2 + c, 1), :] = ids[pl.ds(m, 1), :]
    own_id = col_ids.at[z, pl.ds(xh * 2 + c, 1)]
    send(own_id, own_id, s_i.at[0], r_i.at[0], x_far)
    send(own_id, own_id, s_i.at[1], r_i.at[1], sibling)
    part_f[0] = project(q_p)
    e_send[1, hi_h, :] = part_f[0, hi_h, :].astype(BF16)
    exchange_direct(0, e_send, e_recv, s_e, r_e)
    part_f[1] = project(q_m)
    e_send[2, lo_h, :] = part_f[1, lo_h, :].astype(BF16)
    exchange_direct(1, e_send, e_recv, s_e, r_e)
    part_own[...] = project(m)
    recv(col_ids.at[z, pl.ds((1 - xh) * 2 + c, 1)], r_i.at[0])
    recv(col_ids.at[z, pl.ds(xh * 2 + 1 - c, 1)], r_i.at[1])
    far_id = col_ids.at[z, pl.ds((1 - xh) * 2 + c, 1)]
    send(far_id, far_id, s_i.at[2], r_i.at[2], sibling)
    exchange_sum(0, e_send, e_opp, e_recv, s_e, r_e, part_f[0, lo_h, :])
    exchange_sum(1, e_send, e_opp, e_recv, s_e, r_e, part_f[1, hi_h, :])
    recv(col_ids.at[z, pl.ds((1 - xh) * 2 + 1 - c, 1)], r_i.at[2])

    def ids_ring(s):
        send(col_ids.at[zoff(-s)], col_ids.at[zoff(-s)], s_i.at[3 + 2 * s], r_i.at[3 + 2 * s], z_dev[0])
        if s < 3:
            send(col_ids.at[zoff(s)], col_ids.at[zoff(s)], s_i.at[4 + 2 * s], r_i.at[4 + 2 * s], z_dev[1])

    def ids_wait(s):
        recv(col_ids.at[zoff(-1 - s)], r_i.at[3 + 2 * s])
        if s < 3:
            recv(col_ids.at[zoff(1 + s)], r_i.at[4 + 2 * s])

    ids_ring(0)
    for q in range(4):
        row_ids[pl.ds(q * Q, Q), :] = jnp.transpose(jnp.broadcast_to(ids[pl.ds(q, 1), :], (Q, Q)))
    ids_wait(0)
    ids_ring(1)
    j = lax.broadcasted_iota(I32, (512, 448), 0)
    i = lax.broadcasted_iota(I32, (512, 448), 1)
    r = jnp.bitwise_and(j, 15)
    dest = (
        jnp.bitwise_and(jnp.right_shift(j, 4), 1) * 16
        + jnp.bitwise_and(jnp.right_shift(j, 5), 7) * 2
        + jnp.right_shift(j, 8)
    )
    sel[...] = jnp.where((i == dest * 14 + r) & (r < 14), 1.0, 0.0).astype(BF16)
    ids_wait(1)
    ids_ring(2)
    xpad[...] = lax.dot_general(sel[...], x[...], NT, preferred_element_type=F32).astype(BF16)
    ids_wait(2)
    ids_ring(3)
    acc[...] = jnp.zeros_like(acc)
    lacc[...] = jnp.zeros_like(lacc)
    ids_wait(3)

    emb = exchange_total(e_recv, r_e, part_own[...])
    inv = lax.rsqrt(jnp.sum(emb * emb, axis=1, keepdims=True) + NORM_EPS)
    inv_own[...] = jnp.broadcast_to(inv, (Q, Q))
    uvec = emb * inv
    unit_own[...] = uvec
    unit[rows_of(m), :] = uvec.astype(BF16)

    own_rows = unit.at[rows_of(m)]
    own_lo, own_hi = unit.at[rows_of(m, 0, H)], unit.at[rows_of(m, H, H)]

    def block(z_, xh_, c_, half):
        return cols.at[z_, pl.ds(pl.multiple_of((xh_ * 2 + c_) * Q + half * H, H), H)]

    def ring_send(k, s, src):
        zz = zoff(-s) if k == 0 else zoff(s)
        if s < 3:
            send(src, ring.at[zz], s_z2.at[k, s], r_z2.at[k, s], z_dev[k])
        else:
            part = pl.ds(k * 32, 32)
            send(src.at[part], ring.at[zz, part], s_z2.at[k, s], r_z2.at[k, s], z_dev[k])

    def ring_recv(k, s):
        zz = zoff(-s) if k == 0 else zoff(s)
        if s < 4:
            recv(ring.at[zz], r_z2.at[k, s - 1])
        else:
            part = pl.ds(k * 32, 32)
            recv(ring.at[zz, part], r_z2.at[k, s - 1])

    def across(zz, src):
        dst = block(zz, xh, c, 1)
        send(src, dst, s_x2.at[zz, 0], r_x2.at[zz, 0], x_same)
        send(src, dst, s_x2.at[zz, 1], r_x2.at[zz, 1], x_other)

    def across_recv(zz):
        for k in range(2):
            xk = xh if k == 0 else 1 - xh
            b = block(zz, xk, c, 1)
            recv(b, r_x2.at[zz, k])
            send(b, b, s_sib.at[zz, xk, 1], r_sib.at[zz, xk, 1], sibling)

    def to_sibling(zz, xk):
        b = block(zz, xk, c, 0)
        send(b, b, s_sib.at[zz, xk, 0], r_sib.at[zz, xk, 0], sibling)

    def from_sibling(zz):
        for xk in range(2):
            for half in range(2):
                recv(block(zz, xk, 1 - c, half), r_sib.at[zz, xk, half])

    def z_send(k, s, xk):
        zz = zoff(-s) if k == 0 else zoff(s)
        b = block(zz, xk, c, 0)
        send(b, b, s_z1.at[k, s, xk], r_z1.at[k, s, xk], z_dev[k])

    def z_recv(k, s, xk):
        zz = zoff(-s) if k == 0 else zoff(s)
        recv(block(zz, xk, c, 0), r_z1.at[k, s - 1, xk])

    ring_send(0, 0, own_hi)
    ring_send(1, 0, own_hi)
    send(own_lo, block(z, xh, c, 0), s_x1.at[0], r_x1.at[0], x_same)
    send(own_lo, block(z, xh, c, 0), s_x1.at[1], r_x1.at[1], x_other)
    across(z, own_hi)
    send(own_rows, own_rows, s_u.at[0], r_u.at[0], y_dev[0])
    send(own_rows, own_rows, s_u.at[1], r_u.at[1], y_dev[1])
    for k in range(2):
        xk = xh if k == 0 else 1 - xh
        recv(block(z, xk, c, 0), r_x1.at[k])
    for xk in range(2):
        for k in range(2):
            z_send(k, 0, xk)
        to_sibling(z, xk)
    across_recv(z)
    def pair_unit(zz):
        from_sibling(zz)

        def tile(rt, carry):
            rows = pl.ds(pl.multiple_of(rt * 256, 256), 256)
            logits[...] = lax.dot_general(unit[rows, :], cols[zz], NT, preferred_element_type=F32)

            def chunk(ci, carry):
                lr = pl.ds(pl.multiple_of(ci * 16, 16), 16)
                ar = pl.ds(pl.multiple_of(rt * 256 + ci * 16, 16), 16)
                rid = row_ids[ar, :]
                total = lacc[ar, :]
                for jj in range(4):
                    cc = pl.ds(jj * 128, 128)
                    same = rid == col_ids[zz, pl.ds(jj, 1), :]
                    lg = logits[lr, cc] * (LOGIT_SCALE * LOG2E) + (LOGIT_BIAS * LOG2E)
                    v = jnp.where(same, -lg, lg)
                    e = jnp.exp2(-jnp.abs(v))
                    u = 1.0 + e
                    lg1 = jnp.where(e < 2.0**-12, e * LOG2E, jnp.log2(u))
                    total = total + (jnp.maximum(v, 0.0) + lg1)
                    sg = jnp.where(v >= 0.0, 1.0, e) / u
                    slope[lr, cc] = jnp.where(same, -sg, sg).astype(BF16)
                lacc[ar, :] = total
                return carry

            lax.fori_loop(0, 16, chunk, 0, unroll=2)
            acc[rows, :] += jnp.dot(slope[...], cols[zz], preferred_element_type=F32)
            return carry

        lax.fori_loop(0, 2, tile, 0)

    def pair_units(s):
        if s in (0, 4):
            pair_unit(zoff(s))
        else:
            for k in range(2):
                pair_unit(zoff(s if k else -s))

    for s in range(1, 5):
        ks = range(2)
        for k in ks:
            ring_recv(k, s)
            if s < 4:
                zz = zoff(s if k else -s)
                ring_send(k, s, ring.at[zz])
                across(zz, ring.at[zz])
        if s == 4:
            across(zoff(4), ring.at[zoff(4)])
        for xk in range(2):
            for k in ks:
                if s < 4:
                    z_recv(k, s, xk)
                    if s < 3 or xk == k:
                        z_send(k, s, xk)
                    to_sibling(zoff(s if k else -s), xk)
                elif xk == k:
                    z_recv(k, s, xk)
                    to_sibling(zoff(4), xk)
        if s == 1:
            recv(unit.at[rows_of(q_m)], r_u.at[0])
            fwd = unit.at[rows_of(q_m, 0, H)]
            send(fwd, fwd, s_u.at[2], r_u.at[2], y_dev[0])
            recv(unit.at[rows_of(q_p)], r_u.at[1])
            fwd = unit.at[rows_of(q_p, H, H)]
            send(fwd, fwd, s_u.at[3], r_u.at[3], y_dev[1])
        if s == 2:
            recv(unit.at[rows_of(q_opp, 0, H)], r_u.at[2])
            recv(unit.at[rows_of(q_opp, H, H)], r_u.at[3])
            pair_units(0)
        if s > 1:
            pair_units(s - 1)
        if s < 4:
            across_recv(zoff(-s))
            across_recv(zoff(s))
        else:
            across_recv(zoff(4))
    pair_units(4)

    for q, b in ((q_opp, 0), (q_p, 1), (q_m, 2)):
        if b == 0:
            g_send[0] = acc[rows_of(q), :].astype(BF16)
            exchange_opposite(g_send, g_opp, s_g, r_g)
        else:
            half, lo = (hi_h, H) if b == 1 else (lo_h, 0)
            g_send[b, half, :] = acc[rows_of(q, lo, H), :].astype(BF16)
            exchange_direct(b - 1, g_send, g_recv, s_g, r_g)
    for q in range(4):
        col = jnp.transpose(lacc[pl.ds(q * Q, Q), :])
        loss_v[m, pl.ds(q, 1), :] = jnp.sum(col, axis=0, keepdims=True)
    send(loss_v.at[m], loss_v.at[m], s_l.at[0], r_l.at[0], y_dev[0])
    send(loss_v.at[m], loss_v.at[m], s_l.at[1], r_l.at[1], y_dev[1])
    exchange_sum(0, g_send, g_opp, g_recv, s_g, r_g, acc[rows_of(q_p, 0, H), :])
    exchange_sum(1, g_send, g_opp, g_recv, s_g, r_g, acc[rows_of(q_m, H, H), :])
    recv(loss_v.at[q_m], r_l.at[0])
    send(loss_v.at[q_m], loss_v.at[q_m], s_l.at[2], r_l.at[2], y_dev[0])
    recv(loss_v.at[q_p], r_l.at[1])
    recv(loss_v.at[q_opp], r_l.at[2])
    loss_out[...] = (loss_v[0] + loss_v[1] + loss_v[2] + loss_v[3]) * (LN2 / (512 * 32))
    ug = exchange_total(g_recv, r_g, acc[rows_of(m), :]) * LOGIT_SCALE
    uvec = unit_own[...]
    inner = jnp.sum(uvec * ug, axis=1, keepdims=True)
    delta[rows_of(m), :] = ((ug - uvec * inner) * inv_own[:, 0:1]).astype(BF16)

    def grad_rows(q):
        dx_out[rows_of(q), :] = lax.dot_general(
            delta[rows_of(q), :], w[...], NT, preferred_element_type=F32
        ).astype(BF16)

    own_delta = delta.at[rows_of(m)]
    send(own_delta, own_delta, s_d.at[0], r_d.at[0], y_dev[0])
    send(own_delta, own_delta, s_d.at[1], r_d.at[1], y_dev[1])
    grad_rows(m)
    recv(delta.at[rows_of(q_m)], r_d.at[0])
    fwd = delta.at[rows_of(q_m, 0, H)]
    send(fwd, fwd, s_d.at[2], r_d.at[2], y_dev[0])
    recv(delta.at[rows_of(q_p)], r_d.at[1])
    fwd = delta.at[rows_of(q_p, H, H)]
    send(fwd, fwd, s_d.at[3], r_d.at[3], y_dev[1])
    grad_rows(q_m)
    grad_rows(q_p)
    recv(delta.at[rows_of(q_opp, 0, H)], r_d.at[2])
    recv(delta.at[rows_of(q_opp, H, H)], r_d.at[3])

    for k in range(2):
        cc = 1 - c if k == 0 else c
        rows = pl.ds(pl.multiple_of(cc * 256, 256), 256)
        dw_acc[k] = jnp.dot(xpad[rows, :], delta[...], preferred_element_type=F32)
        if k == 0:
            sib_dw[0] = dw_acc[0].astype(BF16)
            send(sib_dw.at[0], sib_dw.at[1], s_w.at[0], r_w.at[0], sibling)
    grad_rows(q_opp)
    recv(sib_dw.at[1], r_w.at[0])
    dw_acc[1] += sib_dw[1].astype(F32)

    def dest_rows(k, lo=0, n=32):
        return pl.ds(pl.multiple_of(zoff(k) * 32 + lo, 16), n)

    for s in range(4):
        for k in range(2):
            off = (4 - s) if k == 0 else (s - 4)
            if s == 0:
                part = pl.ds(0, 16)
                zs_send[k, 0, part, :] = dw_acc[1, dest_rows(off, 16 * k, 16), :].astype(BF16)
                send(zs_send.at[k, 0, part], zs_recv.at[k, 0, part], s_w.at[1 + k], r_w.at[1 + k], z_dev[k])
                continue
            own = dw_acc[1, dest_rows(off), :]
            if s == 1:
                part = pl.ds(0, 16)
                recv(zs_recv.at[k, 0, part], r_w.at[1 + k])
                got = zs_recv[k, 0, part, :].astype(F32)
                for hx in range(2):
                    v = own[16 * hx : 16 * hx + 16]
                    zs_send[k, 1, pl.ds(16 * hx, 16), :] = (v + got if hx == k else v).astype(BF16)
            else:
                recv(zs_recv.at[k, s - 1], r_w.at[2 * s - 1 + k])
                zs_send[k, s] = (own + zs_recv[k, s - 1].astype(F32)).astype(BF16)
            send(zs_send.at[k, s], zs_recv.at[k, s], s_w.at[2 * s + 1 + k], r_w.at[2 * s + 1 + k], z_dev[k])
    for k in range(2):
        recv(zs_recv.at[k, 3], r_w.at[7 + k])

    def total_rows(xk):
        part = pl.ds(pl.multiple_of(xk * 16, 16), 16)
        return (
            dw_acc[1, pl.ds(pl.multiple_of(z * 32 + xk * 16, 16), 16), :]
            + zs_recv[0, 3, part, :].astype(F32)
            + zs_recv[1, 3, part, :].astype(F32)
        )

    x_send[...] = total_rows(1 - xh).astype(BF16)
    send(x_send, x_recv, s_w.at[9], r_w.at[9], x_far)
    own = total_rows(xh)
    recv(x_recv, r_w.at[9])
    dw_out[...] = (own + x_recv[...].astype(F32))[:14]
    for copy in sends:
        copy.wait_send()


def local(inputs, weights, pair_ids):
    V = pltpu.VMEM
    dma = pltpu.SemaphoreType.DMA
    scratch = [
        V((512, E), BF16), V((Q, E), F32), V((Q, Q), F32), V((2, Q, E), F32), V((Q, E), F32),
        V((3, Q, E), BF16), V((2, H, E), BF16), V((2, Q, E), BF16),
        V((8, 512, E), BF16), V((8, H, E), BF16), V((8, 4, 128), I32), V((512, 128), I32),
        V((512, 448), BF16), V((512, 512), BF16), V((256, 512), F32), V((256, 512), BF16),
        V((512, E), F32), V((512, 128), F32),
        V((3, Q, E), BF16), V((2, H, E), BF16), V((2, Q, E), BF16),
        V((4, 4, 128), F32), V((512, E), BF16), V((2, 256, E), F32), V((2, 256, E), BF16),
        V((2, 4, 32, E), BF16), V((2, 4, 32, E), BF16), V((16, E), BF16), V((16, E), BF16),
    ]
    for shape in (
        (6,), (10,), (4,), (2,), (2, 4, 2), (2, 4), (8, 2), (8, 2, 2), (6,), (3,), (4,), (10,)
    ):
        scratch += [dma(shape), dma(shape)]
    vmem = pl.BlockSpec(memory_space=pltpu.VMEM)
    loss, dx, dw = pl.pallas_call(
        kernel,
        out_shape=(
            jax.ShapeDtypeStruct((4, 128), F32),
            jax.ShapeDtypeStruct((512, 448), BF16),
            jax.ShapeDtypeStruct((14, E), F32),
        ),
        in_specs=[vmem] * 3,
        out_specs=(vmem,) * 3,
        scratch_shapes=scratch,
        compiler_params=pltpu.CompilerParams(
            collective_id=0, has_side_effects=True, vmem_limit_bytes=56 * 2**20
        ),
        cost_estimate=pl.CostEstimate(flops=11 * 10**9, bytes_accessed=2 * 10**6, transcendentals=6 * 10**6),
    )(inputs[0], weights[0], pair_ids.reshape(4, 128))
    return loss.reshape(1, 512), dx[None], dw[None]


def solution(mesh):
    return jax.shard_map(
        local,
        mesh=mesh,
        in_specs=(P("tower", "dp", "mp"), P("tower", "mp", None), P("dp")),
        out_specs=(P("tower", "dp"), P("tower", "dp", "mp"), P("tower", ("mp", "dp"), None)),
        check_vma=False,
    )
```

time: 393 us -> 134 us (0.34)
  waiting for transfers between devices: 202 us -> 0 us
  blocking collectives: 127 us -> 0 us
  Pallas kernels: 0 us -> 126 us
  matrix products: 27.7 us -> 0 us
  between operations: 14.6 us -> 0.65 us
  starting transfers between devices: 8.74 us -> 0 us
  other arithmetic: 5.48 us -> 0 us
    pallas_call x0 -> x1, Pallas kernels: none -> 126 us  [local(): pl.pallas_call(kernel, out_shape=(jax.ShapeDtypeStruct((4, 128), F32), ja...]
    psum x2 -> x0, waiting for transfers between devices: 124 us -> none  [the longest x1 71.1 us: local(): embedding = lax.psum(partial_value, 'mp')]
    unnamed x1 -> x0, blocking collectives: 76.1 us -> none
    all_gather x1 -> x0, waiting for transfers between devices: 63.3 us -> none  [local(): partner_block = lax.all_gather(partner, 'dp', axis=0, tiled=True)]
    all_gather x1 -> x0, blocking collectives: 40.4 us -> none  [local(): other_ids = lax.all_gather(mine_ids, 'dp', axis=0, tiled=True)]
    dot_general x5 -> x0, matrix products: 27.7 us -> none  [the longest x1 12.5 us: pair_terms(): jnp.dot(local_unit_rows, partner_unit_rows.T, preferred_element_type=jnp....]
    psum x1 -> x0, blocking collectives: 10.5 us -> none  [local(): unit_grad, loss_total = lax.psum((local_gradient, loss_own), 'mp')]
    ppermute x1 -> x0, waiting for transfers between devices: 8 us -> none  [partner_2(): lax.ppermute(array, axis, [(i, i ^ 1 << stride) for i in range(lax.axis_s...]
  transfers between devices with their start and end apart: 8 -> 0, of which waited for: 5 -> 0; matrix products, arithmetic and copies ran while one was open for 1% -> 0% of each run, Pallas kernels for 0% -> 0%
where the time goes in v1:
time: 134 us; the launch traced here: 132 us
  Pallas kernels  126 us (94%)
  local copies, waits for them, and re-layouts  5.33 us (4%)
    pallas_call x1, Pallas kernels, local(): pl.pallas_call(kernel, out_shape=(jax.ShapeDtypeStruct((4, 128), F32), ja...  126 us
    unnamed x8, local copies, waits for them, and re-layouts  5.33 us

profile of v1, /device:TPU:6, one launch (start us, length us, event | category | flops | bytes accessed | tf_op | source)
XLA Modules:
  0.0 132.1 jit_solution(7901308783248533913)
XLA Ops:
  0.6 2.0 %copy.6 = bf16[1,512,448]{2,1,0:T(8,128)(2,1)} copy(bf16[1,512,448]{1,2,0:T(8,128)(2,1)} %param.3) | data formatting | bytes 917504 | tf_op args[0]
  2.6 126.2 %shard_map.58 = (f32[4,128]{1,0:T(4,128)}, bf16[512,448]{1,0:T(8,128)(2,1)}, f32[14,1152]{1,0:T(8,128)}) custom-call(bf16[512,448]{1,0:T(8,128)(2,1)} %bitcast.7, bf16[448,1152]{1,0:T(8,128)(2,1)} %bitcast.10, s32[4,128]{1,0:T(4,128)} %bitcast.11), custom_call_target="tpu_custom_call" | custom-call | flops 11000000512 | bytes 2000000 | tf_op jit(solution)/shard_map/pallas_call | solution.py:426
  128.8 0.0 copy-start
  128.8 2.0 %copy.7 = bf16[1,512,448]{1,2,0:T(8,128)(2,1)} copy(bf16[1,512,448]{2,1,0:T(8,128)(2,1)} %bitcast.6) | data formatting | bytes 917504
  130.9 0.0 copy-done
  130.9 0.0 copy-start.1
  130.9 0.7 copy.8
  131.6 0.0 copy-done.1
  131.6 0.6 copy.10
Async XLA Ops:
  128.8 2.0 %copy-start = (f32[14,1152]{1,0:T(8,128)S(1)}, f32[14,1152]{1,0:T(8,128)}, u32[]{:S(2)}) copy-start(f32[14,1152]{1,0:T(8,128)} %get-tuple-element.8) | copy-start | bytes 193540
  130.9 0.7 copy-start.1

commit v2 on v0

v2 whole, which is shorter than its diff:
```python
import jax
import jax.numpy as jnp
from jax import lax
from jax.experimental import pallas as pl
from jax.experimental.pallas import tpu as pltpu
from jax.sharding import PartitionSpec as P

MESH = pl.DeviceIdType.MESH
F32, BF16, I32 = jnp.float32, jnp.bfloat16, jnp.int32
LOGIT_SCALE = 100.0
LOGIT_BIAS = -6.0
NORM_EPS = 1e-06
LOG2E = 1.4426950408889634
LN2 = 0.6931471805599453

E = 1152
Q = 128
H = 64
W = 32
CHUNKS = ((0, 512), (512, 384), (896, 256))
NT = (((1,), (1,)), ((), ()))
TN = (((0,), (0,)), ((), ()))


def kernel(xt, w, ids, loss_out, dx_out, dw_out, *scratch):
    (
        unit, unit_own, inv_own, part_f,
        e_send, e_opp, e_recv,
        cols, ring, col_ids, row_ids, sel, xpad, logits, slope, acc, lacc,
        g_send, g_opp, g_recv,
        loss_v, delta, dw_own, sib_dw, dw_send, dw_recv,
        s_a, s_z, s_x2, s_sib, s_b, s_i, s_l,
        r_e, r_g, r_i, r_u, r_x1, r_z1, r_z2, r_x2, r_sib, r_l, r_d0, r_d1, r_df, r_ws, r_w,
    ) = scratch
    t, d, m = lax.axis_index("tower"), lax.axis_index("dp"), lax.axis_index("mp")
    c, z, xh = lax.rem(d, 2), lax.rem(d // 2, 8), d // 16

    def at_dp(xh_, z_, c_):
        return (xh_ * 8 + z_) * 2 + c_

    def zoff(k):
        return lax.rem(z + (k + 8), 8)

    def moff(k):
        return lax.rem(m + (k + 4), 4)

    x_same, x_other = (1 - t, d, m), (1 - t, at_dp(1 - xh, z, c), m)
    y_dev = ((t, d, moff(1)), (t, d, moff(-1)))
    sibling = (t, at_dp(xh, z, 1 - c), m)
    far = {
        (dz, dx): (t, at_dp(1 - xh if dx else xh, zoff(dz), c), m)
        for dz in range(8) for dx in range(2) if dz or dx
    }
    z_dev = (far[1, 0], far[7, 0])
    x_far = far[0, 1]
    others = (x_same, x_other, *y_dev, sibling, *far.values())

    def send(src, dst, ss, rs, dev):
        pltpu.make_async_remote_copy(
            src_ref=src, dst_ref=dst, send_sem=ss, recv_sem=rs, device_id=dev, device_id_type=MESH
        ).start()

    def share(ref, ss, rs, dev):
        send(ref, ref, ss, rs, dev)

    def recv(dst, rs):
        pltpu.make_async_remote_copy(
            src_ref=dst, dst_ref=dst, send_sem=rs, recv_sem=rs, device_id=sibling, device_id_type=MESH
        ).wait_recv()

    def sent(ref, ss):
        pltpu.make_async_remote_copy(
            src_ref=ref, dst_ref=ref, send_sem=ss, recv_sem=ss, device_id=sibling, device_id_type=MESH
        ).wait_send()

    def rows_of(q, lo=0, n=Q):
        return pl.ds(pl.multiple_of(q * Q + lo, 16), n)

    q_opp, q_p, q_m = moff(2), moff(1), moff(-1)

    barrier = pltpu.get_barrier_semaphore()
    for dev in others:
        pl.semaphore_signal(barrier, inc=1, device_id=dev, device_id_type=MESH)

    def project(q):
        cc = pl.ds(pl.multiple_of(q * Q, Q), Q)
        return lax.dot_general(xt[:, cc], w[...], TN, preferred_element_type=F32)

    e_send[0] = project(q_opp).astype(BF16)
    pl.semaphore_wait(barrier, len(others))

    def part(h, k):
        return pl.ds(h * H + k * W, W)

    def rs_opposite(h, buf, opp, ss, rs):
        for k in range(2):
            send(buf.at[0, part(h, k)], opp.at[h, k], ss, rs.at[h, 0, k], y_dev[k])

    def rs_direct(h, k, buf, got, ss, rs):
        p = part(h, 1 - k)
        send(buf.at[1 + k, p], got.at[k, p], ss, rs.at[h, 1, k], y_dev[k])

    def rs_sum(h, k, buf, opp, got, ss, rs, own):
        p = part(h, k)
        recv(opp.at[h, k], rs.at[h, 0, k])
        buf[1 + k, p, :] = (own + opp[h, k].astype(F32)).astype(BF16)
        send(buf.at[1 + k, p], got.at[k, p], ss, rs.at[h, 2, k], y_dev[k])

    def rs_total(h, got, rs, own):
        for k in range(2):
            recv(got.at[k, part(h, 1 - k)], rs.at[h, 1, k])
            recv(got.at[k, part(h, k)], rs.at[h, 2, k])
        rows = pl.ds(h * H, H)
        return own + got[0, rows, :].astype(F32) + got[1, rows, :].astype(F32)

    def id_row(dc, dx):
        cc = 1 - c if dc else c
        xx = 1 - xh if dx else xh
        return col_ids.at[z, pl.ds(cc * 2 + xx, 1)]

    col_ids[z, pl.ds(c * 2 + xh, 1), :] = ids[pl.ds(m, 1), :]
    share(id_row(0, 0), s_i.at[0], r_i.at[0], x_far)
    share(id_row(0, 0), s_i.at[0], r_i.at[1], sibling)

    def ids_ring(s):
        share(col_ids.at[zoff(-s)], s_i.at[1], r_i.at[3 + 2 * s], z_dev[0])
        if s < 3:
            share(col_ids.at[zoff(s)], s_i.at[1], r_i.at[4 + 2 * s], z_dev[1])

    def ids_wait(s):
        recv(col_ids.at[zoff(-1 - s)], r_i.at[3 + 2 * s])
        if s < 3:
            recv(col_ids.at[zoff(1 + s)], r_i.at[4 + 2 * s])

    for h in range(2):
        rs_opposite(h, e_send, e_opp, s_a, r_e)
    for k, q in ((0, q_p), (1, q_m)):
        part_f[k] = project(q)
        p = part(0, 1 - k)
        e_send[1 + k, p, :] = part_f[k, p, :].astype(BF16)
        rs_direct(0, k, e_send, e_recv, s_a, r_e)
    part_f[2] = project(m)
    for h in range(2):
        if h:
            for k in range(2):
                p = part(1, 1 - k)
                e_send[1 + k, p, :] = part_f[k, p, :].astype(BF16)
                rs_direct(1, k, e_send, e_recv, s_a, r_e)
        for k in range(2):
            rs_sum(h, k, e_send, e_opp, e_recv, s_a, r_e, part_f[k, part(h, k), :])
    recv(id_row(0, 1), r_i.at[0])
    recv(id_row(1, 0), r_i.at[1])
    share(id_row(0, 1), s_i.at[0], r_i.at[2], sibling)

    for q in range(4):
        row_ids[pl.ds(q * Q, Q), :] = jnp.transpose(jnp.broadcast_to(ids[pl.ds(q, 1), :], (Q, Q)))
    j = lax.broadcasted_iota(I32, (512, 448), 0)
    i = lax.broadcasted_iota(I32, (512, 448), 1)
    r = jnp.bitwise_and(j, 15)
    dest = (
        jnp.bitwise_and(jnp.right_shift(j, 4), 1) * 16
        + jnp.bitwise_and(jnp.right_shift(j, 5), 7) * 2
        + jnp.right_shift(j, 8)
    )
    sel[...] = jnp.where((i == dest * 14 + r) & (r < 14), 1.0, 0.0).astype(BF16)
    xpad[...] = jnp.dot(sel[...], xt[...], preferred_element_type=F32).astype(BF16)
    acc[...] = jnp.zeros_like(acc)
    lacc[...] = jnp.zeros_like(lacc)
    recv(id_row(1, 1), r_i.at[2])
    ids_ring(0)

    def normalise(h):
        rows = pl.ds(h * H, H)
        emb = rs_total(h, e_recv, r_e, part_f[2, rows, :])
        inv = lax.rsqrt(jnp.sum(emb * emb, axis=1, keepdims=True) + NORM_EPS)
        inv_own[rows, :] = jnp.broadcast_to(inv, (H, Q))
        uvec = emb * inv
        unit_own[rows, :] = uvec
        unit[rows_of(m, h * H, H), :] = uvec.astype(BF16)

    def block(z_, xh_, c_, half):
        return cols.at[pl.ds(pl.multiple_of(((z_ * 2 + c_) * 2 + xh_) * Q + half * H, H), H)]

    def unit_rows(q, h):
        return unit.at[rows_of(q, h * H, H)]

    def ring_send(k, s, src):
        zz = zoff(-s) if k == 0 else zoff(s)
        if s < 3:
            send(src, ring.at[zz], s_z, r_z2.at[k, s], z_dev[k])
        else:
            p = pl.ds(k * W, W)
            send(src.at[p], ring.at[zz, p], s_z, r_z2.at[k, s], z_dev[k])

    def ring_recv(k, s):
        zz = zoff(-s) if k == 0 else zoff(s)
        if s < 4:
            recv(ring.at[zz], r_z2.at[k, s - 1])
        else:
            recv(ring.at[zz, pl.ds(k * W, W)], r_z2.at[k, s - 1])

    def across(zz, src):
        dst = block(zz, xh, c, 1)
        send(src, dst, s_x2, r_x2.at[zz, 0], x_same)
        send(src, dst, s_x2, r_x2.at[zz, 1], x_other)

    def across_recv(zz):
        for k in range(2):
            b = block(zz, xh if k == 0 else 1 - xh, c, 1)
            recv(b, r_x2.at[zz, k])
            share(b, s_sib, r_sib.at[zz], sibling)

    def to_sibling(zz, xk):
        share(block(zz, xk, c, 0), s_sib, r_sib.at[zz], sibling)

    def z_send(k, s, xk):
        share(block(zoff(-s if k == 0 else s), xk, c, 0), s_z, r_z1.at[k, s, xk], z_dev[k])

    def z_recv(k, s, xk):
        recv(block(zoff(-s if k == 0 else s), xk, c, 0), r_z1.at[k, s - 1, xk])

    normalise(0)
    own = unit_rows(m, 0)
    send(own, block(z, xh, c, 0), s_a, r_x1.at[0], x_same)
    send(own, block(z, xh, c, 0), s_a, r_x1.at[1], x_other)
    for k in range(2):
        share(own, s_a, r_u.at[0, k], y_dev[k])
    ids_wait(0)
    ids_ring(1)
    normalise(1)
    own = unit_rows(m, 1)
    for k in range(2):
        ring_send(k, 0, own)
    across(z, own)
    for k in range(2):
        share(own, s_a, r_u.at[1, k], y_dev[k])
    ids_wait(1)
    ids_ring(2)
    for k in range(2):
        recv(block(z, xh if k == 0 else 1 - xh, c, 0), r_x1.at[k])
    for xk in range(2):
        for k in range(2):
            z_send(k, 0, xk)
    for xk in range(2):
        to_sibling(z, xk)

    def pair_tile(zz, start, n):
        rows = pl.ds(pl.multiple_of(start, n), n)
        cc = pl.ds(pl.multiple_of(zz * 512, 512), 512)
        lr_all = pl.ds(0, n)
        logits[lr_all, :] = lax.dot_general(unit[rows, :], cols[cc, :], NT, preferred_element_type=F32)

        def chunk(ci, carry):
            lr = pl.ds(pl.multiple_of(ci * 16, 16), 16)
            ar = pl.ds(pl.multiple_of(start + ci * 16, 16), 16)
            rid = row_ids[ar, :]
            total = lacc[ar, :]
            for jj in range(4):
                lc = pl.ds(jj * 128, 128)
                same = rid == col_ids[zz, pl.ds(jj, 1), :]
                lg = logits[lr, lc] * (LOGIT_SCALE * LOG2E) + (LOGIT_BIAS * LOG2E)
                v = jnp.where(same, -lg, lg)
                e = jnp.exp2(-jnp.abs(v))
                u = 1.0 + e
                lg1 = jnp.where(e < 2.0**-12, e * LOG2E, jnp.log2(u))
                total = total + (jnp.maximum(v, 0.0) + lg1)
                sg = jnp.where(v >= 0.0, 1.0, e) / u
                slope[lr, lc] = jnp.where(same, -sg, sg).astype(BF16)
            lacc[ar, :] = total
            return carry

        lax.fori_loop(0, n // 16, chunk, 0, unroll=2)
        acc[rows, :] += jnp.dot(slope[lr_all, :], cols[cc, :], preferred_element_type=F32)

    def from_sibling(zz):
        rows = pl.ds(pl.multiple_of((zz * 2 + 1 - c) * 2 * Q, 2 * Q), 2 * Q)
        recv(cols.at[rows], r_sib.at[zz])

    done = [0]

    def tiles(n):
        def tile(ti, carry):
            u, rt = ti // 2, lax.rem(ti, 2)
            dist = (u + 1) // 2
            zz = lax.rem(z + jnp.where(lax.rem(u, 2) == 1, dist, 8 - dist), 8)

            @pl.when(rt == 0)
            def _():
                from_sibling(zz)

            pair_tile(zz, rt * 256, 256)
            return carry

        lax.fori_loop(done[0], done[0] + n, tile, 0)
        done[0] += n

    slots = {2: (2, 2, 1, 1), 3: (1, 1, 1, 1), 4: (2, 1, 1, 0)}
    for s in range(1, 5):
        dist = (s,) if s == 4 else (-s, s)
        run = slots.get(s, (0, 0, 0, 0))
        if s < 3:
            ids_wait(s + 1)
            if s == 1:
                ids_ring(3)
        for k in range(2):
            ring_recv(k, s)
            if s < 4:
                ring_send(k, s, ring.at[zoff(dist[k])])
        for ds_ in dist:
            across(zoff(ds_), ring.at[zoff(ds_)])
        if s == 1:
            across_recv(z)
            recv(unit_rows(q_m, 0), r_u.at[0, 0])
            share(unit_rows(q_m, 0), s_a, r_u.at[2, 0], y_dev[0])
            recv(unit_rows(q_p, 0), r_u.at[0, 1])
        if s == 2:
            recv(unit_rows(q_m, 1), r_u.at[1, 0])
            recv(unit_rows(q_opp, 0), r_u.at[2, 0])
            recv(unit_rows(q_opp, 1), r_u.at[2, 1])
        if run[0]:
            tiles(run[0])
        for xk in range(2):
            for k in range(2):
                if s < 4:
                    z_recv(k, s, xk)
                    if s < 3 or xk == k:
                        z_send(k, s, xk)
                elif xk == k:
                    z_recv(k, s, xk)
            for k in range(len(dist)):
                to_sibling(zoff(dist[k]), xk)
            if run[1 + xk]:
                tiles(run[1 + xk])
            if s == 1 and xk == 0:
                recv(unit_rows(q_p, 1), r_u.at[1, 1])
                share(unit_rows(q_p, 1), s_a, r_u.at[2, 1], y_dev[1])
        for ds_ in dist:
            across_recv(zoff(ds_))
        if run[3]:
            tiles(run[3])

    z_last = zoff(4)
    from_sibling(z_last)
    pair_tile(z_last, q_opp * Q, Q)
    g_send[0] = acc[rows_of(q_opp), :].astype(BF16)
    for h in range(2):
        rs_opposite(h, g_send, g_opp, s_b, r_g)
    for k, q in ((0, q_p), (1, q_m)):
        pair_tile(z_last, q * Q, Q)
        g_send[1 + k, part(0, 1 - k), :] = acc[rows_of(q, (1 - k) * W, W), :].astype(BF16)
        rs_direct(0, k, g_send, g_recv, s_b, r_g)
    pair_tile(z_last, m * Q, Q)
    for q in range(4):
        col = jnp.transpose(lacc[pl.ds(q * Q, Q), :])
        loss_v[m, pl.ds(q, 1), :] = jnp.sum(col, axis=0, keepdims=True)
    for h in range(2):
        if h:
            for k, q in ((0, q_p), (1, q_m)):
                g_send[1 + k, part(1, 1 - k), :] = acc[rows_of(q, H + (1 - k) * W, W), :].astype(BF16)
                rs_direct(1, k, g_send, g_recv, s_b, r_g)
        for k, q in ((0, q_p), (1, q_m)):
            rs_sum(h, k, g_send, g_opp, g_recv, s_b, r_g, acc[rows_of(q, h * H + k * W, W), :])
    for k in range(2):
        share(loss_v.at[m], s_l, r_l.at[k], y_dev[k])

    def back(h):
        rows = pl.ds(h * H, H)
        ug = rs_total(h, g_recv, r_g, acc[rows_of(m, h * H, H), :]) * LOGIT_SCALE
        uvec = unit_own[rows, :]
        inner = jnp.sum(uvec * ug, axis=1, keepdims=True)
        delta[rows_of(m, h * H, H), :] = ((ug - uvec * inner) * inv_own[rows, 0:1]).astype(BF16)

    def delta_rows(q, h, e=None):
        rows = rows_of(q, h * H, H)
        return delta.at[rows] if e is None else delta.at[rows, pl.ds(*CHUNKS[e])]

    def grad_rows(q):
        dx_out[:, pl.ds(pl.multiple_of(q * Q, Q), Q)] = lax.dot_general(
            w[...], delta[rows_of(q), :], NT, preferred_element_type=F32
        ).astype(BF16)

    back(0)
    for k in range(2):
        share(delta_rows(m, 0), s_b, r_d0.at[k], y_dev[k])
    back(1)
    for e in range(3):
        for k in range(2):
            share(delta_rows(m, 1, e), s_b, r_d1.at[k, e], y_dev[k])
    grad_rows(m)
    recv(delta_rows(q_m, 0), r_d0.at[0])
    for e in range(3):
        share(delta_rows(q_m, 0, e), s_b, r_df.at[0, e], y_dev[0])
    recv(loss_v.at[q_m], r_l.at[0])
    share(loss_v.at[q_m], s_l, r_l.at[2], y_dev[0])
    for e in range(3):
        recv(delta_rows(q_p, 1, e), r_d1.at[1, e])
        share(delta_rows(q_p, 1, e), s_b, r_df.at[1, e], y_dev[1])
    recv(delta_rows(q_p, 0), r_d0.at[1])
    grad_rows(q_p)
    for e in range(3):
        recv(delta_rows(q_m, 1, e), r_d1.at[0, e])
    grad_rows(q_m)

    def dw_products(e):
        cc = pl.ds(*CHUNKS[e])
        recv(delta_rows(q_opp, 0, e), r_df.at[0, e])
        recv(delta_rows(q_opp, 1, e), r_df.at[1, e])
        for dc in range(2):
            rows = pl.ds(pl.multiple_of((c if dc else 1 - c) * 256, 256), 256)
            prod = jnp.dot(xpad[rows, :], delta[:, cc], preferred_element_type=F32)
            if dc:
                dw_own[:, cc] = prod
            else:
                sib_dw[0, :, cc] = prod.astype(BF16)
                send(sib_dw.at[0, :, cc], sib_dw.at[1, :, cc], s_b, r_ws.at[e], sibling)

    def dest_rows(dz, dx):
        xx = 1 - xh if dx else xh
        return pl.ds(pl.multiple_of((zoff(dz) * 2 + xx) * 16, 16), 16)

    def dw_exchange(e):
        cc = pl.ds(*CHUNKS[e])
        recv(sib_dw.at[1, :, cc], r_ws.at[e])
        both = dw_own[:, cc] + sib_dw[1, :, cc].astype(F32)
        dw_own[:, cc] = both
        dw_send[:, cc] = both.astype(BF16)
        for n, (dz, dx) in enumerate(far):
            send(
                dw_send.at[dest_rows(dz, dx), cc], dw_recv.at[pl.ds(n * 16, 16), cc],
                s_b, r_w.at[e], far[dz, dx],
            )

    dw_products(0)
    dw_products(1)
    dw_exchange(0)
    dw_products(2)
    dw_exchange(1)
    dw_exchange(2)
    grad_rows(q_opp)
    recv(loss_v.at[q_p], r_l.at[1])
    recv(loss_v.at[q_opp], r_l.at[2])
    loss = (loss_v[0] + loss_v[1] + loss_v[2] + loss_v[3]) * (LN2 / (512 * 32))
    for q in range(4):
        loss_out[:, pl.ds(q * Q, Q)] = loss[q : q + 1]
    for e in range(3):
        cc = pl.ds(*CHUNKS[e])
        recv(dw_recv.at[:, cc], r_w.at[e])
        total = dw_own[dest_rows(0, 0), cc]
        for n in range(15):
            total = total + dw_recv[pl.ds(n * 16, 16), cc].astype(F32)
        for row in range(14):
            dw_out[row, :, cc] = total[row : row + 1]
    for ss, n in ((s_a, 384 + 128 + 384), (s_z, 14 * 64 + 448), (s_x2, 1024), (s_sib, 2048), (s_b, 384 + 384 + 256 + 240)):
        sent(cols.at[pl.ds(0, n)], ss)
    sent(col_ids.at[0, pl.ds(0, 3)], s_i.at[0])
    sent(col_ids.at[pl.ds(0, 7)], s_i.at[1])
    sent(loss_v.at[pl.ds(0, 3)], s_l)


def local(inputs, weights, pair_ids):
    V = pltpu.VMEM
    dma = pltpu.SemaphoreType.DMA
    scratch = [
        V((512, E), BF16), V((Q, E), F32), V((Q, Q), F32), V((3, Q, E), F32),
        V((3, Q, E), BF16), V((2, 2, W, E), BF16), V((2, Q, E), BF16),
        V((4096, E), BF16), V((8, H, E), BF16), V((8, 4, 128), I32), V((512, 128), I32),
        V((512, 448), BF16), V((512, 512), BF16), V((256, 512), F32), V((256, 512), BF16),
        V((512, E), F32), V((512, 128), F32),
        V((3, Q, E), BF16), V((2, 2, W, E), BF16), V((2, Q, E), BF16),
        V((4, 4, 128), F32), V((512, E), BF16), V((256, E), F32), V((2, 256, E), BF16),
        V((256, E), BF16), V((240, E), BF16),
    ]
    for shape in (
        (), (), (), (), (), (2,), (),
        (2, 3, 2), (2, 3, 2), (10,), (3, 2), (2,), (2, 4, 2), (2, 4), (8, 2), (8,), (3,),
        (2,), (2, 3), (2, 3), (3,), (3,),
    ):
        scratch.append(dma(shape))
    vmem = pl.BlockSpec(memory_space=pltpu.VMEM)
    loss, dx, dw = pl.pallas_call(
        kernel,
        out_shape=(
            jax.ShapeDtypeStruct((1, 512), F32),
            jax.ShapeDtypeStruct((448, 512), BF16),
            jax.ShapeDtypeStruct((14, 1, E), F32),
        ),
        in_specs=[vmem] * 3,
        out_specs=(vmem,) * 3,
        scratch_shapes=scratch,
        compiler_params=pltpu.CompilerParams(
            collective_id=0, has_side_effects=True, vmem_limit_bytes=56 * 2**20
        ),
        cost_estimate=pl.CostEstimate(flops=11 * 10**9, bytes_accessed=2 * 10**6, transcendentals=6 * 10**6),
    )(jnp.swapaxes(inputs[0], 0, 1), weights[0], pair_ids.reshape(4, 128))
    return loss, jnp.swapaxes(dx, 0, 1)[None], dw.reshape(1, 14, E)


def solution(mesh):
    return jax.shard_map(
        local,
        mesh=mesh,
        in_specs=(P("tower", "dp", "mp"), P("tower", "mp", None), P("dp")),
        out_specs=(P("tower", "dp"), P("tower", "dp", "mp"), P("tower", ("mp", "dp"), None)),
        check_vma=False,
    )
```

time: 393 us -> 113 us (0.29)
  waiting for transfers between devices: 202 us -> 0 us
  blocking collectives: 127 us -> 0 us
  Pallas kernels: 0 us -> 108 us
  matrix products: 27.7 us -> 0 us
  between operations: 14.6 us -> 0.65 us
  starting transfers between devices: 8.74 us -> 0 us
  other arithmetic: 5.48 us -> 0 us
    psum x2 -> x0, waiting for transfers between devices: 124 us -> none  [the longest x1 71.1 us: local(): embedding = lax.psum(partial_value, 'mp')]
    pallas_call x0 -> x1, Pallas kernels: none -> 108 us  [local(): pl.pallas_call(kernel, out_shape=(jax.ShapeDtypeStruct((1, 512), F32), ja...]
    unnamed x1 -> x0, blocking collectives: 76.1 us -> none
    all_gather x1 -> x0, waiting for transfers between devices: 63.3 us -> none  [local(): partner_block = lax.all_gather(partner, 'dp', axis=0, tiled=True)]
    all_gather x1 -> x0, blocking collectives: 40.4 us -> none  [local(): other_ids = lax.all_gather(mine_ids, 'dp', axis=0, tiled=True)]
    dot_general x5 -> x0, matrix products: 27.7 us -> none  [the longest x1 12.5 us: pair_terms(): jnp.dot(local_unit_rows, partner_unit_rows.T, preferred_element_type=jnp....]
    psum x1 -> x0, blocking collectives: 10.5 us -> none  [local(): unit_grad, loss_total = lax.psum((local_gradient, loss_own), 'mp')]
    ppermute x1 -> x0, waiting for transfers between devices: 8 us -> none  [partner_2(): lax.ppermute(array, axis, [(i, i ^ 1 << stride) for i in range(lax.axis_s...]
  transfers between devices with their start and end apart: 8 -> 0, of which waited for: 5 -> 0; matrix products, arithmetic and copies ran while one was open for 1% -> 0% of each run, Pallas kernels for 0% -> 0%
where the time goes in v2:
time: 113 us; the launch traced here: 112 us
  Pallas kernels  108 us (96%)
  local copies, waits for them, and re-layouts  3.68 us (3%)
    pallas_call x1, Pallas kernels, local(): pl.pallas_call(kernel, out_shape=(jax.ShapeDtypeStruct((1, 512), F32), ja...  108 us
    unnamed x7, local copies, waits for them, and re-layouts  3.68 us

profile of v2, /device:TPU:6, one launch (start us, length us, event | category | flops | bytes accessed | tf_op | source)
XLA Modules:
  0.0 112.5 jit_solution(16041736459053290835)
XLA Ops:
  0.6 108.1 %shard_map.58 = (f32[1,512]{1,0:T(1,128)}, bf16[448,512]{1,0:T(8,128)(2,1)}, f32[14,1,1152]{2,1,0:T(1,128)}) custom-call(bf16[448,512]{1,0:T(8,128)(2,1)} %bitcast.12, bf16[448,1152]{1,0:T(8,128)(2,1)} %bitcast.11, s32[4,128]{1,0:T(4,128)} %bitcast.13), custom_call_target="tpu_custom_call" | custom-call | flops 11000000512 | bytes 2000000 | tf_op jit(solution)/shard_map/pallas_call | solution.py:480
  108.8 0.0 copy-start.1
  108.8 0.7 copy-done.1
  109.4 0.6 copy.9
  110.0 0.0 copy-start
  110.0 1.8 %copy.10 = bf16[1,512,448]{1,2,0:T(8,128)(2,1)} copy(bf16[1,512,448]{1,2,0:T(8,128)(2,1)} %bitcast.9) | data formatting | bytes 917504
  111.8 0.0 copy-done
  111.9 0.6 copy.11
Async XLA Ops:
  108.8 0.7 copy-start.1
  110.0 1.8 %copy-start = (f32[14,1,1152]{2,1,0:T(1,128)S(1)}, f32[14,1,1152]{2,1,0:T(1,128)}, u32[]{:S(2)}) copy-start(f32[14,1,1152]{2,1,0:T(1,128)} %get-tuple-element.8) | copy-start | bytes 193540

commit v3 on v2

--- a/solution.py
+++ b/solution.py
@@ -17,7 +17,8 @@
 Q = 128
 H = 64
 W = 32
-CHUNKS = ((0, 512), (512, 384), (896, 256))
+V = 16
+CHUNKS = ((0, 384), (384, 384), (768, 384))
 NT = (((1,), (1,)), ((), ()))
 TN = (((0,), (0,)), ((), ()))
 
@@ -28,9 +29,9 @@
         e_send, e_opp, e_recv,
         cols, ring, col_ids, row_ids, sel, xpad, logits, slope, acc, lacc,
         g_send, g_opp, g_recv,
-        loss_v, delta, dw_own, sib_dw, dw_send, dw_recv,
+        loss_v, delta, dw_own, sib_dw, dw_send, dw_recv, dx_recv,
         s_a, s_z, s_x2, s_sib, s_b, s_i, s_l,
-        r_e, r_g, r_i, r_u, r_x1, r_z1, r_z2, r_x2, r_sib, r_l, r_d0, r_d1, r_df, r_ws, r_w,
+        r_e, r_g, r_i, r_u, r_x1, r_z0, r_z1, r_z2, r_x2, r_sib, r_l, r_d0, r_d1, r_df, r_ws, r_wx, r_w,
     ) = scratch
     t, d, m = lax.axis_index("tower"), lax.axis_index("dp"), lax.axis_index("mp")
     c, z, xh = lax.rem(d, 2), lax.rem(d // 2, 8), d // 16
@@ -49,7 +50,7 @@
     sibling = (t, at_dp(xh, z, 1 - c), m)
     far = {
         (dz, dx): (t, at_dp(1 - xh if dx else xh, zoff(dz), c), m)
-        for dz in range(8) for dx in range(2) if dz or dx
+        for dx in range(2) for dz in range(8) if dz or dx
     }
     z_dev = (far[1, 0], far[7, 0])
     x_far = far[0, 1]
@@ -89,28 +90,29 @@
     e_send[0] = project(q_opp).astype(BF16)
     pl.semaphore_wait(barrier, len(others))
 
-    def part(h, k):
-        return pl.ds(h * H + k * W, W)
+    def part(h, k, n):
+        return pl.ds((2 * h + k) * n, n)
 
     def rs_opposite(h, buf, opp, ss, rs):
-        for k in range(2):
-            send(buf.at[0, part(h, k)], opp.at[h, k], ss, rs.at[h, 0, k], y_dev[k])
-
-    def rs_direct(h, k, buf, got, ss, rs):
-        p = part(h, 1 - k)
+        n = opp.shape[2]
+        for k in range(2):
+            send(buf.at[0, part(h, k, n)], opp.at[h, k], ss, rs.at[h, 0, k], y_dev[k])
+
+    def rs_direct(h, k, buf, got, ss, rs, n):
+        p = part(h, 1 - k, n)
         send(buf.at[1 + k, p], got.at[k, p], ss, rs.at[h, 1, k], y_dev[k])
 
     def rs_sum(h, k, buf, opp, got, ss, rs, own):
-        p = part(h, k)
+        p = part(h, k, opp.shape[2])
         recv(opp.at[h, k], rs.at[h, 0, k])
         buf[1 + k, p, :] = (own + opp[h, k].astype(F32)).astype(BF16)
         send(buf.at[1 + k, p], got.at[k, p], ss, rs.at[h, 2, k], y_dev[k])
 
-    def rs_total(h, got, rs, own):
-        for k in range(2):
-            recv(got.at[k, part(h, 1 - k)], rs.at[h, 1, k])
-            recv(got.at[k, part(h, k)], rs.at[h, 2, k])
-        rows = pl.ds(h * H, H)
+    def rs_total(h, got, rs, own, n):
+        for k in range(2):
+            recv(got.at[k, part(h, 1 - k, n)], rs.at[h, 1, k])
+            recv(got.at[k, part(h, k, n)], rs.at[h, 2, k])
+        rows = pl.ds(2 * h * n, 2 * n)
         return own + got[0, rows, :].astype(F32) + got[1, rows, :].astype(F32)
 
     def id_row(dc, dx):
@@ -132,22 +134,18 @@
         if s < 3:
             recv(col_ids.at[zoff(1 + s)], r_i.at[4 + 2 * s])
 
-    for h in range(2):
+    for h in range(4):
         rs_opposite(h, e_send, e_opp, s_a, r_e)
     for k, q in ((0, q_p), (1, q_m)):
         part_f[k] = project(q)
-        p = part(0, 1 - k)
-        e_send[1 + k, p, :] = part_f[k, p, :].astype(BF16)
-        rs_direct(0, k, e_send, e_recv, s_a, r_e)
+    for h in range(4):
+        for k in range(2):
+            p = part(h, 1 - k, V)
+            e_send[1 + k, p, :] = part_f[k, p, :].astype(BF16)
+            rs_direct(h, k, e_send, e_recv, s_a, r_e, V)
+        for k in range(2):
+            rs_sum(h, k, e_send, e_opp, e_recv, s_a, r_e, part_f[k, part(h, k, V), :])
     part_f[2] = project(m)
-    for h in range(2):
-        if h:
-            for k in range(2):
-                p = part(1, 1 - k)
-                e_send[1 + k, p, :] = part_f[k, p, :].astype(BF16)
-                rs_direct(1, k, e_send, e_recv, s_a, r_e)
-        for k in range(2):
-            rs_sum(h, k, e_send, e_opp, e_recv, s_a, r_e, part_f[k, part(h, k), :])
     recv(id_row(0, 1), r_i.at[0])
     recv(id_row(1, 0), r_i.at[1])
     share(id_row(0, 1), s_i.at[0], r_i.at[2], sibling)
@@ -158,8 +156,8 @@
     i = lax.broadcasted_iota(I32, (512, 448), 1)
     r = jnp.bitwise_and(j, 15)
     dest = (
-        jnp.bitwise_and(jnp.right_shift(j, 4), 1) * 16
-        + jnp.bitwise_and(jnp.right_shift(j, 5), 7) * 2
+        jnp.bitwise_and(jnp.right_shift(j, 7), 1) * 16
+        + jnp.bitwise_and(jnp.right_shift(j, 4), 7) * 2
         + jnp.right_shift(j, 8)
     )
     sel[...] = jnp.where((i == dest * 14 + r) & (r < 14), 1.0, 0.0).astype(BF16)
@@ -170,77 +168,86 @@
     ids_ring(0)
 
     def normalise(h):
-        rows = pl.ds(h * H, H)
-        emb = rs_total(h, e_recv, r_e, part_f[2, rows, :])
+        rows = pl.ds(h * W, W)
+        emb = rs_total(h, e_recv, r_e, part_f[2, rows, :], V)
         inv = lax.rsqrt(jnp.sum(emb * emb, axis=1, keepdims=True) + NORM_EPS)
-        inv_own[rows, :] = jnp.broadcast_to(inv, (H, Q))
+        inv_own[rows, :] = jnp.broadcast_to(inv, (W, Q))
         uvec = emb * inv
         unit_own[rows, :] = uvec
-        unit[rows_of(m, h * H, H), :] = uvec.astype(BF16)
-
-    def block(z_, xh_, c_, half):
-        return cols.at[pl.ds(pl.multiple_of(((z_ * 2 + c_) * 2 + xh_) * Q + half * H, H), H)]
+        unit[rows_of(m, h * W, W), :] = uvec.astype(BF16)
+
+    def block(z_, xh_, c_, lo, n):
+        return cols.at[pl.ds(pl.multiple_of(((z_ * 2 + c_) * 2 + xh_) * Q + lo, 16), n)]
 
     def unit_rows(q, h):
         return unit.at[rows_of(q, h * H, H)]
 
-    def ring_send(k, s, src):
-        zz = zoff(-s) if k == 0 else zoff(s)
-        if s < 3:
-            send(src, ring.at[zz], s_z, r_z2.at[k, s], z_dev[k])
-        else:
-            p = pl.ds(k * W, W)
-            send(src.at[p], ring.at[zz, p], s_z, r_z2.at[k, s], z_dev[k])
-
-    def ring_recv(k, s):
-        zz = zoff(-s) if k == 0 else zoff(s)
+    def ring_send(k, s, p, src):
+        if s < 3 or p == k:
+            zz = zoff(-s if k == 0 else s)
+            send(src, ring.at[zz, pl.ds(p * W, W)], s_z, r_z2.at[k, s, p], z_dev[k])
+
+    def ring_recv(k, s, p):
+        zz = zoff(-s if k == 0 else s)
+        piece = ring.at[zz, pl.ds(p * W, W)]
+        if s < 4 or p == k:
+            recv(piece, r_z2.at[k, s - 1, p])
         if s < 4:
-            recv(ring.at[zz], r_z2.at[k, s - 1])
-        else:
-            recv(ring.at[zz, pl.ds(k * W, W)], r_z2.at[k, s - 1])
+            ring_send(k, s, p, piece)
 
     def across(zz, src):
-        dst = block(zz, xh, c, 1)
+        dst = block(zz, xh, c, 0, H)
         send(src, dst, s_x2, r_x2.at[zz, 0], x_same)
         send(src, dst, s_x2, r_x2.at[zz, 1], x_other)
 
     def across_recv(zz):
         for k in range(2):
-            b = block(zz, xh if k == 0 else 1 - xh, c, 1)
+            b = block(zz, xh if k == 0 else 1 - xh, c, 0, H)
             recv(b, r_x2.at[zz, k])
             share(b, s_sib, r_sib.at[zz], sibling)
 
     def to_sibling(zz, xk):
-        share(block(zz, xk, c, 0), s_sib, r_sib.at[zz], sibling)
+        share(block(zz, xk, c, H, H), s_sib, r_sib.at[zz], sibling)
+
+    def z_first(p):
+        for k in range(2):
+            recv(block(z, xh if k == 0 else 1 - xh, c, H + p * W, W), r_x1.at[k, p])
+        for xk in range(2):
+            for k in range(2):
+                share(block(z, xk, c, H + p * W, W), s_z, r_z0.at[k, xk, p], z_dev[k])
 
     def z_send(k, s, xk):
-        share(block(zoff(-s if k == 0 else s), xk, c, 0), s_z, r_z1.at[k, s, xk], z_dev[k])
+        share(block(zoff(-s if k == 0 else s), xk, c, H, H), s_z, r_z1.at[k, s - 1, xk], z_dev[k])
 
     def z_recv(k, s, xk):
-        recv(block(zoff(-s if k == 0 else s), xk, c, 0), r_z1.at[k, s - 1, xk])
-
-    normalise(0)
-    own = unit_rows(m, 0)
-    send(own, block(z, xh, c, 0), s_a, r_x1.at[0], x_same)
-    send(own, block(z, xh, c, 0), s_a, r_x1.at[1], x_other)
-    for k in range(2):
-        share(own, s_a, r_u.at[0, k], y_dev[k])
-    ids_wait(0)
-    ids_ring(1)
-    normalise(1)
-    own = unit_rows(m, 1)
-    for k in range(2):
-        ring_send(k, 0, own)
-    across(z, own)
-    for k in range(2):
-        share(own, s_a, r_u.at[1, k], y_dev[k])
-    ids_wait(1)
-    ids_ring(2)
-    for k in range(2):
-        recv(block(z, xh if k == 0 else 1 - xh, c, 0), r_x1.at[k])
-    for xk in range(2):
-        for k in range(2):
-            z_send(k, 0, xk)
+        zz = zoff(-s if k == 0 else s)
+        if s == 1:
+            for p in range(2):
+                recv(block(zz, xk, c, H + p * W, W), r_z0.at[k, xk, p])
+        else:
+            recv(block(zz, xk, c, H, H), r_z1.at[k, s - 2, xk])
+
+    for h in range(4):
+        normalise(h)
+        own = unit.at[rows_of(m, h * W, W)]
+        if h < 2:
+            for k in range(2):
+                ring_send(k, 0, h, own)
+        else:
+            dst = block(z, xh, c, h * W, W)
+            send(own, dst, s_a, r_x1.at[0, h - 2], x_same)
+            send(own, dst, s_a, r_x1.at[1, h - 2], x_other)
+        if h % 2:
+            for k in range(2):
+                share(unit_rows(m, h // 2), s_a, r_u.at[h // 2, k], y_dev[k])
+            ids_wait(h // 2)
+            ids_ring(h // 2 + 1)
+    across(z, unit_rows(m, 0))
+    for p in range(2):
+        for k in range(2):
+            ring_recv(k, 1, p)
+    for p in range(2):
+        z_first(p)
     for xk in range(2):
         to_sibling(z, xk)
 
@@ -302,10 +309,10 @@
             ids_wait(s + 1)
             if s == 1:
                 ids_ring(3)
-        for k in range(2):
-            ring_recv(k, s)
-            if s < 4:
-                ring_send(k, s, ring.at[zoff(dist[k])])
+        if s > 1:
+            for p in range(2):
+                for k in range(2):
+                    ring_recv(k, s, p)
         for ds_ in dist:
             across(zoff(ds_), ring.at[zoff(ds_)])
         if s == 1:
@@ -347,8 +354,8 @@
         rs_opposite(h, g_send, g_opp, s_b, r_g)
     for k, q in ((0, q_p), (1, q_m)):
         pair_tile(z_last, q * Q, Q)
-        g_send[1 + k, part(0, 1 - k), :] = acc[rows_of(q, (1 - k) * W, W), :].astype(BF16)
-        rs_direct(0, k, g_send, g_recv, s_b, r_g)
+        g_send[1 + k, part(0, 1 - k, W), :] = acc[rows_of(q, (1 - k) * W, W), :].astype(BF16)
+        rs_direct(0, k, g_send, g_recv, s_b, r_g, W)
     pair_tile(z_last, m * Q, Q)
     for q in range(4):
         col = jnp.transpose(lacc[pl.ds(q * Q, Q), :])
@@ -356,8 +363,8 @@
     for h in range(2):
         if h:
             for k, q in ((0, q_p), (1, q_m)):
-                g_send[1 + k, part(1, 1 - k), :] = acc[rows_of(q, H + (1 - k) * W, W), :].astype(BF16)
-                rs_direct(1, k, g_send, g_recv, s_b, r_g)
+                g_send[1 + k, part(1, 1 - k, W), :] = acc[rows_of(q, H + (1 - k) * W, W), :].astype(BF16)
+                rs_direct(1, k, g_send, g_recv, s_b, r_g, W)
         for k, q in ((0, q_p), (1, q_m)):
             rs_sum(h, k, g_send, g_opp, g_recv, s_b, r_g, acc[rows_of(q, h * H + k * W, W), :])
     for k in range(2):
@@ -365,7 +372,7 @@
 
     def back(h):
         rows = pl.ds(h * H, H)
-        ug = rs_total(h, g_recv, r_g, acc[rows_of(m, h * H, H), :]) * LOGIT_SCALE
+        ug = rs_total(h, g_recv, r_g, acc[rows_of(m, h * H, H), :], W) * LOGIT_SCALE
         uvec = unit_own[rows, :]
         inner = jnp.sum(uvec * ug, axis=1, keepdims=True)
         delta[rows_of(m, h * H, H), :] = ((ug - uvec * inner) * inv_own[rows, 0:1]).astype(BF16)
@@ -414,28 +421,46 @@
                 sib_dw[0, :, cc] = prod.astype(BF16)
                 send(sib_dw.at[0, :, cc], sib_dw.at[1, :, cc], s_b, r_ws.at[e], sibling)
 
+    def x_rows(dx):
+        return pl.ds(pl.multiple_of((1 - xh if dx else xh) * 128, 128), 128)
+
     def dest_rows(dz, dx):
-        xx = 1 - xh if dx else xh
-        return pl.ds(pl.multiple_of((zoff(dz) * 2 + xx) * 16, 16), 16)
-
-    def dw_exchange(e):
+        return pl.ds(pl.multiple_of(((1 - xh if dx else xh) * 8 + zoff(dz)) * 16, 16), 16)
+
+    slots_of = {dest: pl.ds(n * 16, 16) for n, dest in enumerate(far)}
+
+    def dw_cores(e):
         cc = pl.ds(*CHUNKS[e])
         recv(sib_dw.at[1, :, cc], r_ws.at[e])
         both = dw_own[:, cc] + sib_dw[1, :, cc].astype(F32)
         dw_own[:, cc] = both
         dw_send[:, cc] = both.astype(BF16)
-        for n, (dz, dx) in enumerate(far):
-            send(
-                dw_send.at[dest_rows(dz, dx), cc], dw_recv.at[pl.ds(n * 16, 16), cc],
-                s_b, r_w.at[e], far[dz, dx],
-            )
+        if e < 2:
+            send(dw_send.at[x_rows(1), cc], dx_recv.at[:, cc], s_b, r_wx.at[e], x_far)
+        else:
+            dw_out_of(e, far)
+
+    def dw_x(e):
+        cc = pl.ds(*CHUNKS[e])
+        recv(dx_recv.at[:, cc], r_wx.at[e])
+        both = dw_own[x_rows(0), cc] + dx_recv[:, cc].astype(F32)
+        dw_own[x_rows(0), cc] = both
+        dw_send[x_rows(0), cc] = both.astype(BF16)
+        dw_out_of(e, [dest for dest in far if not dest[1]])
+
+    def dw_out_of(e, dests):
+        cc = pl.ds(*CHUNKS[e])
+        for dest in dests:
+            send(dw_send.at[dest_rows(*dest), cc], dw_recv.at[slots_of[dest], cc], s_b, r_w.at[e], far[dest])
 
     dw_products(0)
     dw_products(1)
-    dw_exchange(0)
+    dw_cores(0)
     dw_products(2)
-    dw_exchange(1)
-    dw_exchange(2)
+    dw_cores(1)
+    dw_cores(2)
+    dw_x(0)
+    dw_x(1)
     grad_rows(q_opp)
     recv(loss_v.at[q_p], r_l.at[1])
     recv(loss_v.at[q_opp], r_l.at[2])
@@ -444,9 +469,10 @@
         loss_out[:, pl.ds(q * Q, Q)] = loss[q : q + 1]
     for e in range(3):
         cc = pl.ds(*CHUNKS[e])
-        recv(dw_recv.at[:, cc], r_w.at[e])
+        n_in = 7 if e < 2 else 15
+        recv(dw_recv.at[pl.ds(0, n_in * 16), cc], r_w.at[e])
         total = dw_own[dest_rows(0, 0), cc]
-        for n in range(15):
+        for n in range(n_in):
             total = total + dw_recv[pl.ds(n * 16, 16), cc].astype(F32)
         for row in range(14):
             dw_out[row, :, cc] = total[row : row + 1]
@@ -457,27 +483,32 @@
     sent(loss_v.at[pl.ds(0, 3)], s_l)
 
 
+def hand_out(*refs):
+    for n in range(3):
+        refs[3 + n][...] = refs[n][...]
+
+
 def local(inputs, weights, pair_ids):
-    V = pltpu.VMEM
+    A = pltpu.VMEM
     dma = pltpu.SemaphoreType.DMA
     scratch = [
-        V((512, E), BF16), V((Q, E), F32), V((Q, Q), F32), V((3, Q, E), F32),
-        V((3, Q, E), BF16), V((2, 2, W, E), BF16), V((2, Q, E), BF16),
-        V((4096, E), BF16), V((8, H, E), BF16), V((8, 4, 128), I32), V((512, 128), I32),
-        V((512, 448), BF16), V((512, 512), BF16), V((256, 512), F32), V((256, 512), BF16),
-        V((512, E), F32), V((512, 128), F32),
-        V((3, Q, E), BF16), V((2, 2, W, E), BF16), V((2, Q, E), BF16),
-        V((4, 4, 128), F32), V((512, E), BF16), V((256, E), F32), V((2, 256, E), BF16),
-        V((256, E), BF16), V((240, E), BF16),
+        A((512, E), BF16), A((Q, E), F32), A((Q, Q), F32), A((3, Q, E), F32),
+        A((3, Q, E), BF16), A((4, 2, V, E), BF16), A((2, Q, E), BF16),
+        A((4096, E), BF16), A((8, H, E), BF16), A((8, 4, 128), I32), A((512, 128), I32),
+        A((512, 448), BF16), A((512, 512), BF16), A((256, 512), F32), A((256, 512), BF16),
+        A((512, E), F32), A((512, 128), F32),
+        A((3, Q, E), BF16), A((2, 2, W, E), BF16), A((2, Q, E), BF16),
+        A((4, 4, 128), F32), A((512, E), BF16), A((256, E), F32), A((2, 256, E), BF16),
+        A((256, E), BF16), A((240, E), BF16), A((128, E), BF16),
     ]
     for shape in (
         (), (), (), (), (), (2,), (),
-        (2, 3, 2), (2, 3, 2), (10,), (3, 2), (2,), (2, 4, 2), (2, 4), (8, 2), (8,), (3,),
-        (2,), (2, 3), (2, 3), (3,), (3,),
+        (4, 3, 2), (2, 3, 2), (10,), (3, 2), (2, 2), (2, 2, 2), (2, 3, 2), (2, 4, 2), (8, 2), (8,), (3,),
+        (2,), (2, 3), (2, 3), (3,), (2,), (3,),
     ):
         scratch.append(dma(shape))
     vmem = pl.BlockSpec(memory_space=pltpu.VMEM)
-    loss, dx, dw = pl.pallas_call(
+    results = pl.pallas_call(
         kernel,
         out_shape=(
             jax.ShapeDtypeStruct((1, 512), F32),
@@ -492,6 +523,12 @@
         ),
         cost_estimate=pl.CostEstimate(flops=11 * 10**9, bytes_accessed=2 * 10**6, transcendentals=6 * 10**6),
     )(jnp.swapaxes(inputs[0], 0, 1), weights[0], pair_ids.reshape(4, 128))
+    loss, dx, dw = pl.pallas_call(
+        hand_out,
+        out_shape=tuple(jax.ShapeDtypeStruct(a.shape, a.dtype) for a in results),
+        in_specs=[vmem] * 3,
+        out_specs=(vmem,) * 3,
+    )(*results)
     return loss, jnp.swapaxes(dx, 0, 1)[None], dw.reshape(1, 14, E)
 
 

time: 113 us -> 107 us (0.947)
  local copies, waits for them, and re-layouts: 3.68 us -> 0 us
  Pallas kernels: 108 us -> 106 us
    unnamed x7 -> x0, local copies, waits for them, and re-layouts: 3.68 us -> none
    pallas_call x1, Pallas kernels: 108 us -> 105 us  [local(): pl.pallas_call(kernel, out_shape=(jax.ShapeDtypeStruct((1, 512), F32), ja...]
    pallas_call x0 -> x1, Pallas kernels: none -> 1.83 us  [local(): pl.pallas_call(hand_out, out_shape=tuple((jax.ShapeDtypeStruct(a.shape, a...]
where the time goes in v3:
time: 107 us
  Pallas kernels  106 us (99%)
    pallas_call x1, Pallas kernels, local(): pl.pallas_call(kernel, out_shape=(jax.ShapeDtypeStruct((1, 512), F32), ja...  105 us

profile of v3, /device:TPU:6, one launch (start us, length us, event | category | flops | bytes accessed | tf_op | source)
XLA Modules:
  0.0 107.1 jit_solution(4773613692718611850)
XLA Ops:
  0.6 104.6 %shard_map.58 = (f32[1,512]{1,0:T(1,128)}, bf16[448,512]{1,0:T(8,128)(2,1)}, f32[14,1,1152]{2,1,0:T(1,128)}) custom-call(bf16[448,512]{1,0:T(8,128)(2,1)} %bitcast.10, bf16[448,1152]{1,0:T(8,128)(2,1)} %bitcast.9, s32[4,128]{1,0:T(4,128)} %bitcast.13), custom_call_target="tpu_custom_call" | custom-call | flops 11000000512 | bytes 2000000 | tf_op jit(solution)/shard_map/pallas_call | solution.py:511
  105.2 1.8 %shard_map.59 = (f32[1,512]{1,0:T(1,128)}, bf16[448,512]{1,0:T(8,128)(2,1)}, f32[14,1,1152]{2,1,0:T(1,128)}) custom-call(f32[1,512]{1,0:T(1,128)} %get-tuple-element.9.refs_0_, bf16[448,512]{1,0:T(8,128)(2,1)} %get-tuple-element.10.refs_1_, f32[14,1,1152]{2,1,0:T(1,128)} %get-tuple-element.11.refs_2_), custom_call_target="tpu_custom_call" | custom-call | tf_op jit(solution)/shard_map/pallas_call | solution.py:526

commit v4 on v3

--- a/solution.py
+++ b/solution.py
@@ -19,12 +19,14 @@
 W = 32
 V = 16
 CHUNKS = ((0, 384), (384, 384), (768, 384))
+X_FIRST = (0, 1)
 NT = (((1,), (1,)), ((), ()))
 TN = (((0,), (0,)), ((), ()))
 
 
-def kernel(xt, w, ids, loss_out, dx_out, dw_out, *scratch):
+def kernel(xt_in, w_in, ids_in, loss_out, dx_out, dw_out, *scratch):
     (
+        xt, w, ids, s_in,
         unit, unit_own, inv_own, part_f,
         e_send, e_opp, e_recv,
         cols, ring, col_ids, row_ids, sel, xpad, logits, slope, acc, lacc,
@@ -79,6 +81,12 @@
 
     q_opp, q_p, q_m = moff(2), moff(1), moff(-1)
 
+    loads = [
+        pltpu.make_async_copy(src, dst, s_in.at[n])
+        for n, (src, dst) in enumerate(((xt_in, xt), (w_in, w), (ids_in, ids)))
+    ]
+    for load in loads:
+        load.start()
     barrier = pltpu.get_barrier_semaphore()
     for dev in others:
         pl.semaphore_signal(barrier, inc=1, device_id=dev, device_id_type=MESH)
@@ -87,6 +95,8 @@
         cc = pl.ds(pl.multiple_of(q * Q, Q), Q)
         return lax.dot_general(xt[:, cc], w[...], TN, preferred_element_type=F32)
 
+    for load in loads:
+        load.wait()
     e_send[0] = project(q_opp).astype(BF16)
     pl.semaphore_wait(barrier, len(others))
 
@@ -212,8 +222,9 @@
     def z_first(p):
         for k in range(2):
             recv(block(z, xh if k == 0 else 1 - xh, c, H + p * W, W), r_x1.at[k, p])
-        for xk in range(2):
+        for i in range(2):
             for k in range(2):
+                xk = (i + k) % 2
                 share(block(z, xk, c, H + p * W, W), s_z, r_z0.at[k, xk, p], z_dev[k])
 
     def z_send(k, s, xk):
@@ -251,119 +262,152 @@
     for xk in range(2):
         to_sibling(z, xk)
 
-    def pair_tile(zz, start, n):
-        rows = pl.ds(pl.multiple_of(start, n), n)
-        cc = pl.ds(pl.multiple_of(zz * 512, 512), 512)
-        lr_all = pl.ds(0, n)
-        logits[lr_all, :] = lax.dot_general(unit[rows, :], cols[cc, :], NT, preferred_element_type=F32)
-
-        def chunk(ci, carry):
-            lr = pl.ds(pl.multiple_of(ci * 16, 16), 16)
-            ar = pl.ds(pl.multiple_of(start + ci * 16, 16), 16)
-            rid = row_ids[ar, :]
-            total = lacc[ar, :]
-            for jj in range(4):
-                lc = pl.ds(jj * 128, 128)
-                same = rid == col_ids[zz, pl.ds(jj, 1), :]
-                lg = logits[lr, lc] * (LOGIT_SCALE * LOG2E) + (LOGIT_BIAS * LOG2E)
-                v = jnp.where(same, -lg, lg)
-                e = jnp.exp2(-jnp.abs(v))
-                u = 1.0 + e
-                lg1 = jnp.where(e < 2.0**-12, e * LOG2E, jnp.log2(u))
-                total = total + (jnp.maximum(v, 0.0) + lg1)
-                sg = jnp.where(v >= 0.0, 1.0, e) / u
-                slope[lr, lc] = jnp.where(same, -sg, sg).astype(BF16)
-            lacc[ar, :] = total
-            return carry
-
-        lax.fori_loop(0, n // 16, chunk, 0, unroll=2)
-        acc[rows, :] += jnp.dot(slope[lr_all, :], cols[cc, :], preferred_element_type=F32)
+    def pair_logits(zz, rows):
+        logits[rows, :] = lax.dot_general(
+            unit[rows, :], cols[unit_cols(zz), :], NT, preferred_element_type=F32
+        )
+
+    def pair_terms(zz, rows):
+        total = lacc[rows, :]
+        rid = row_ids[rows, :]
+        for jj in range(4):
+            lc = pl.ds(jj * 128, 128)
+            same = rid == col_ids[zz, pl.ds(jj, 1), :]
+            lg = logits[rows, lc] * (LOGIT_SCALE * LOG2E) + (LOGIT_BIAS * LOG2E)
+            v = jnp.where(same, -lg, lg)
+            e = jnp.exp2(-jnp.abs(v))
+            u = 1.0 + e
+            lg1 = jnp.where(e < 2.0**-12, e * LOG2E, jnp.log2(u))
+            total = total + (jnp.maximum(v, 0.0) + lg1)
+            sg = jnp.where(v >= 0.0, 1.0, e) / u
+            slope[rows, lc] = jnp.where(same, -sg, sg).astype(BF16)
+        lacc[rows, :] = total
+
+    def pair_grads(zz, rows):
+        acc[rows, :] += jnp.dot(slope[rows, :], cols[unit_cols(zz), :], preferred_element_type=F32)
+
+    def unit_cols(zz):
+        return pl.ds(pl.multiple_of(zz * 512, 512), 512)
 
     def from_sibling(zz):
         rows = pl.ds(pl.multiple_of((zz * 2 + 1 - c) * 2 * Q, 2 * Q), 2 * Q)
         recv(cols.at[rows], r_sib.at[zz])
 
-    done = [0]
-
-    def tiles(n):
-        def tile(ti, carry):
-            u, rt = ti // 2, lax.rem(ti, 2)
-            dist = (u + 1) // 2
-            zz = lax.rem(z + jnp.where(lax.rem(u, 2) == 1, dist, 8 - dist), 8)
-
-            @pl.when(rt == 0)
-            def _():
-                from_sibling(zz)
-
-            pair_tile(zz, rt * 256, 256)
-            return carry
-
-        lax.fori_loop(done[0], done[0] + n, tile, 0)
-        done[0] += n
-
-    slots = {2: (2, 2, 1, 1), 3: (1, 1, 1, 1), 4: (2, 1, 1, 0)}
-    for s in range(1, 5):
-        dist = (s,) if s == 4 else (-s, s)
-        run = slots.get(s, (0, 0, 0, 0))
-        if s < 3:
-            ids_wait(s + 1)
-            if s == 1:
-                ids_ring(3)
-        if s > 1:
-            for p in range(2):
-                for k in range(2):
-                    ring_recv(k, s, p)
-        for ds_ in dist:
-            across(zoff(ds_), ring.at[zoff(ds_)])
-        if s == 1:
-            across_recv(z)
-            recv(unit_rows(q_m, 0), r_u.at[0, 0])
-            share(unit_rows(q_m, 0), s_a, r_u.at[2, 0], y_dev[0])
-            recv(unit_rows(q_p, 0), r_u.at[0, 1])
-        if s == 2:
-            recv(unit_rows(q_m, 1), r_u.at[1, 0])
-            recv(unit_rows(q_opp, 0), r_u.at[2, 0])
-            recv(unit_rows(q_opp, 1), r_u.at[2, 1])
-        if run[0]:
-            tiles(run[0])
-        for xk in range(2):
+    def ring_step(s):
+        for i in range(2):
             for k in range(2):
-                if s < 4:
-                    z_recv(k, s, xk)
-                    if s < 3 or xk == k:
-                        z_send(k, s, xk)
-                elif xk == k:
-                    z_recv(k, s, xk)
-            for k in range(len(dist)):
-                to_sibling(zoff(dist[k]), xk)
-            if run[1 + xk]:
-                tiles(run[1 + xk])
-            if s == 1 and xk == 0:
-                recv(unit_rows(q_p, 1), r_u.at[1, 1])
-                share(unit_rows(q_p, 1), s_a, r_u.at[2, 1], y_dev[1])
-        for ds_ in dist:
-            across_recv(zoff(ds_))
-        if run[3]:
-            tiles(run[3])
+                ring_recv(k, s, (i + k) % 2)
+        for k in range(1 if s == 4 else 2):
+            across(zoff(s if k else -s), ring.at[zoff(s if k else -s)])
+
+    def z_step(s, i):
+        for k in range(2):
+            xk = (i + k) % 2
+            z_recv(k, s, xk)
+            if s < 3 or (s == 3 and xk == k):
+                z_send(k, s, xk)
+        for k in range(2):
+            to_sibling(zoff(s if k else -s), (i + k) % 2)
+
+    def across_step(s):
+        for k in range(1 if s == 4 else 2):
+            across_recv(zoff(s if k else -s))
+
+    ids_wait(2)
+    ids_ring(3)
+    for k in range(2):
+        across(zoff(1 if k else -1), ring.at[zoff(1 if k else -1)])
+    recv(unit_rows(q_m, 0), r_u.at[0, 0])
+    share(unit_rows(q_m, 0), s_a, r_u.at[2, 0], y_dev[0])
+    ring_step(2)
+    across_recv(z)
+    recv(unit_rows(q_p, 1), r_u.at[1, 1])
+    share(unit_rows(q_p, 1), s_a, r_u.at[2, 1], y_dev[1])
+    z_step(1, 0)
+    z_step(1, 1)
+    ids_wait(3)
+    recv(unit_rows(q_p, 0), r_u.at[0, 1])
+    recv(unit_rows(q_m, 1), r_u.at[1, 0])
+    recv(unit_rows(q_opp, 0), r_u.at[2, 0])
+    recv(unit_rows(q_opp, 1), r_u.at[2, 1])
+
+    def pair_unit(u, carry):
+        @pl.when(u == 1)
+        def _():
+            across_step(1)
+            ring_step(3)
+
+        @pl.when(u == 2)
+        def _():
+            z_step(2, 0)
+
+        @pl.when(u == 3)
+        def _():
+            z_step(2, 1)
+            across_step(2)
+
+        @pl.when(u == 4)
+        def _():
+            ring_step(4)
+
+        @pl.when(u == 5)
+        def _():
+            across_step(3)
+            z_step(3, 0)
+            z_step(3, 1)
+
+        dist = (u + 1) // 2
+        zz = lax.rem(z + jnp.where(lax.rem(u, 2) == 1, dist, 8 - dist), 8)
+        from_sibling(zz)
+        halves = pl.ds(0, 256), pl.ds(256, 256)
+        pair_logits(zz, halves[0])
+        pair_logits(zz, halves[1])
+        pair_terms(zz, halves[0])
+        pair_terms(zz, halves[1])
+        pair_grads(zz, halves[0])
+        pair_grads(zz, halves[1])
+        return carry
+
+    lax.fori_loop(0, 7, pair_unit, 0)
+    z_step(4, 0)
+    across_step(4)
 
     z_last = zoff(4)
     from_sibling(z_last)
-    pair_tile(z_last, q_opp * Q, Q)
-    g_send[0] = acc[rows_of(q_opp), :].astype(BF16)
-    for h in range(2):
-        rs_opposite(h, g_send, g_opp, s_b, r_g)
-    for k, q in ((0, q_p), (1, q_m)):
-        pair_tile(z_last, q * Q, Q)
-        g_send[1 + k, part(0, 1 - k, W), :] = acc[rows_of(q, (1 - k) * W, W), :].astype(BF16)
-        rs_direct(0, k, g_send, g_recv, s_b, r_g, W)
-    pair_tile(z_last, m * Q, Q)
+
+    def last_quarter(n, carry):
+        q = lax.rem(m + jnp.where(n == 0, 2, jnp.where(n == 1, 1, jnp.where(n == 2, 3, 0))), 4)
+        rows = rows_of(q)
+        pair_logits(z_last, rows)
+        pair_terms(z_last, rows)
+        pair_grads(z_last, rows)
+
+        @pl.when(n < 3)
+        def _():
+            g_send[n] = acc[rows, :].astype(BF16)
+
+        @pl.when(n == 0)
+        def _():
+            for h in range(2):
+                rs_opposite(h, g_send, g_opp, s_b, r_g)
+
+        @pl.when(n == 1)
+        def _():
+            rs_direct(0, 0, g_send, g_recv, s_b, r_g, W)
+
+        @pl.when(n == 2)
+        def _():
+            rs_direct(0, 1, g_send, g_recv, s_b, r_g, W)
+
+        return carry
+
+    lax.fori_loop(0, 4, last_quarter, 0)
     for q in range(4):
         col = jnp.transpose(lacc[pl.ds(q * Q, Q), :])
         loss_v[m, pl.ds(q, 1), :] = jnp.sum(col, axis=0, keepdims=True)
     for h in range(2):
         if h:
-            for k, q in ((0, q_p), (1, q_m)):
-                g_send[1 + k, part(1, 1 - k, W), :] = acc[rows_of(q, H + (1 - k) * W, W), :].astype(BF16)
+            for k in range(2):
                 rs_direct(1, k, g_send, g_recv, s_b, r_g, W)
         for k, q in ((0, q_p), (1, q_m)):
             rs_sum(h, k, g_send, g_opp, g_recv, s_b, r_g, acc[rows_of(q, h * H + k * W, W), :])
@@ -390,21 +434,21 @@
     for k in range(2):
         share(delta_rows(m, 0), s_b, r_d0.at[k], y_dev[k])
     back(1)
-    for e in range(3):
+    for e in range(len(CHUNKS)):
         for k in range(2):
             share(delta_rows(m, 1, e), s_b, r_d1.at[k, e], y_dev[k])
     grad_rows(m)
     recv(delta_rows(q_m, 0), r_d0.at[0])
-    for e in range(3):
+    for e in range(len(CHUNKS)):
         share(delta_rows(q_m, 0, e), s_b, r_df.at[0, e], y_dev[0])
     recv(loss_v.at[q_m], r_l.at[0])
     share(loss_v.at[q_m], s_l, r_l.at[2], y_dev[0])
-    for e in range(3):
+    for e in range(len(CHUNKS)):
         recv(delta_rows(q_p, 1, e), r_d1.at[1, e])
         share(delta_rows(q_p, 1, e), s_b, r_df.at[1, e], y_dev[1])
     recv(delta_rows(q_p, 0), r_d0.at[1])
     grad_rows(q_p)
-    for e in range(3):
+    for e in range(len(CHUNKS)):
         recv(delta_rows(q_m, 1, e), r_d1.at[0, e])
     grad_rows(q_m)
 
@@ -435,7 +479,7 @@
         both = dw_own[:, cc] + sib_dw[1, :, cc].astype(F32)
         dw_own[:, cc] = both
         dw_send[:, cc] = both.astype(BF16)
-        if e < 2:
+        if e in X_FIRST:
             send(dw_send.at[x_rows(1), cc], dx_recv.at[:, cc], s_b, r_wx.at[e], x_far)
         else:
             dw_out_of(e, far)
@@ -453,23 +497,23 @@
         for dest in dests:
             send(dw_send.at[dest_rows(*dest), cc], dw_recv.at[slots_of[dest], cc], s_b, r_w.at[e], far[dest])
 
-    dw_products(0)
-    dw_products(1)
-    dw_cores(0)
-    dw_products(2)
-    dw_cores(1)
-    dw_cores(2)
-    dw_x(0)
-    dw_x(1)
+    n_chunks = len(CHUNKS)
+    for e in range(n_chunks):
+        dw_products(e)
+        if e:
+            dw_cores(e - 1)
+    dw_cores(n_chunks - 1)
+    for e in X_FIRST:
+        dw_x(e)
     grad_rows(q_opp)
     recv(loss_v.at[q_p], r_l.at[1])
     recv(loss_v.at[q_opp], r_l.at[2])
     loss = (loss_v[0] + loss_v[1] + loss_v[2] + loss_v[3]) * (LN2 / (512 * 32))
     for q in range(4):
         loss_out[:, pl.ds(q * Q, Q)] = loss[q : q + 1]
-    for e in range(3):
+    for e in range(len(CHUNKS)):
         cc = pl.ds(*CHUNKS[e])
-        n_in = 7 if e < 2 else 15
+        n_in = 7 if e in X_FIRST else 15
         recv(dw_recv.at[pl.ds(0, n_in * 16), cc], r_w.at[e])
         total = dw_own[dest_rows(0, 0), cc]
         for n in range(n_in):
@@ -492,10 +536,11 @@
     A = pltpu.VMEM
     dma = pltpu.SemaphoreType.DMA
     scratch = [
+        A((448, 512), BF16), A((448, E), BF16), A((4, 128), I32), dma((3,)),
         A((512, E), BF16), A((Q, E), F32), A((Q, Q), F32), A((3, Q, E), F32),
         A((3, Q, E), BF16), A((4, 2, V, E), BF16), A((2, Q, E), BF16),
         A((4096, E), BF16), A((8, H, E), BF16), A((8, 4, 128), I32), A((512, 128), I32),
-        A((512, 448), BF16), A((512, 512), BF16), A((256, 512), F32), A((256, 512), BF16),
+        A((512, 448), BF16), A((512, 512), BF16), A((512, 512), F32), A((512, 512), BF16),
         A((512, E), F32), A((512, 128), F32),
         A((3, Q, E), BF16), A((2, 2, W, E), BF16), A((2, Q, E), BF16),
         A((4, 4, 128), F32), A((512, E), BF16), A((256, E), F32), A((2, 256, E), BF16),
@@ -504,7 +549,7 @@
     for shape in (
         (), (), (), (), (), (2,), (),
         (4, 3, 2), (2, 3, 2), (10,), (3, 2), (2, 2), (2, 2, 2), (2, 3, 2), (2, 4, 2), (8, 2), (8,), (3,),
-        (2,), (2, 3), (2, 3), (3,), (2,), (3,),
+        (2,), (2, 4), (2, 4), (4,), (4,), (4,),
     ):
         scratch.append(dma(shape))
     vmem = pl.BlockSpec(memory_space=pltpu.VMEM)
@@ -515,7 +560,7 @@
             jax.ShapeDtypeStruct((448, 512), BF16),
             jax.ShapeDtypeStruct((14, 1, E), F32),
         ),
-        in_specs=[vmem] * 3,
+        in_specs=[pl.BlockSpec(memory_space=pl.ANY)] * 3,
         out_specs=(vmem,) * 3,
         scratch_shapes=scratch,
         compiler_params=pltpu.CompilerParams(

time: 107 us -> 104 us (0.972); the launches traced: 107 us -> 103 us
  Pallas kernels: 106 us -> 102 us
    pallas_call x1, Pallas kernels: 105 us -> 100 us  [local(): pl.pallas_call(kernel, out_shape=(jax.ShapeDtypeStruct((1, 512), F32), ja...]
where the time goes in v4:
time: 104 us; the launch traced here: 103 us
  Pallas kernels  102 us (98%)
    pallas_call x1, Pallas kernels, local(): pl.pallas_call(kernel, out_shape=(jax.ShapeDtypeStruct((1, 512), F32), ja...  100 us

profile of v4, /device:TPU:6, one launch (start us, length us, event | category | flops | bytes accessed | tf_op | source)
XLA Modules:
  0.0 102.6 jit_solution(9237959802073087578)
XLA Ops:
  0.6 100.2 %shard_map.58 = (f32[1,512]{1,0:T(1,128)}, bf16[448,512]{1,0:T(8,128)(2,1)}, f32[14,1,1152]{2,1,0:T(1,128)}) custom-call(bf16[448,512]{1,0:T(8,128)(2,1)} %bitcast.10, bf16[448,1152]{1,0:T(8,128)(2,1)} %bitcast.9, s32[4,128]{1,0:T(4,128)} %bitcast.13), custom_call_target="tpu_custom_call" | custom-call | flops 11000000512 | bytes 2000000 | tf_op jit(solution)/shard_map/pallas_call | solution.py:556
  100.8 1.8 %shard_map.59 = (f32[1,512]{1,0:T(1,128)}, bf16[448,512]{1,0:T(8,128)(2,1)}, f32[14,1,1152]{2,1,0:T(1,128)}) custom-call(f32[1,512]{1,0:T(1,128)} %get-tuple-element.9.refs_0_, bf16[448,512]{1,0:T(8,128)(2,1)} %get-tuple-element.10.refs_1_, f32[14,1,1152]{2,1,0:T(1,128)} %get-tuple-element.11.refs_2_), custom_call_target="tpu_custom_call" | custom-call | tf_op jit(solution)/shard_map/pallas_call | solution.py:571

commit v5 on v4

--- a/solution.py
+++ b/solution.py
@@ -349,11 +349,11 @@
         @pl.when(u == 4)
         def _():
             ring_step(4)
+            z_step(3, 0)
 
         @pl.when(u == 5)
         def _():
             across_step(3)
-            z_step(3, 0)
             z_step(3, 1)
 
         dist = (u + 1) // 2
@@ -527,11 +527,6 @@
     sent(loss_v.at[pl.ds(0, 3)], s_l)
 
 
-def hand_out(*refs):
-    for n in range(3):
-        refs[3 + n][...] = refs[n][...]
-
-
 def local(inputs, weights, pair_ids):
     A = pltpu.VMEM
     dma = pltpu.SemaphoreType.DMA
@@ -553,12 +548,12 @@
     ):
         scratch.append(dma(shape))
     vmem = pl.BlockSpec(memory_space=pltpu.VMEM)
-    results = pl.pallas_call(
+    loss, dx, dw = pl.pallas_call(
         kernel,
         out_shape=(
-            jax.ShapeDtypeStruct((1, 512), F32),
-            jax.ShapeDtypeStruct((448, 512), BF16),
-            jax.ShapeDtypeStruct((14, 1, E), F32),
+            pltpu.VMEM((1, 512), F32),
+            pltpu.VMEM((448, 512), BF16),
+            pltpu.VMEM((14, 1, E), F32),
         ),
         in_specs=[pl.BlockSpec(memory_space=pl.ANY)] * 3,
         out_specs=(vmem,) * 3,
@@ -568,12 +563,6 @@
         ),
         cost_estimate=pl.CostEstimate(flops=11 * 10**9, bytes_accessed=2 * 10**6, transcendentals=6 * 10**6),
     )(jnp.swapaxes(inputs[0], 0, 1), weights[0], pair_ids.reshape(4, 128))
-    loss, dx, dw = pl.pallas_call(
-        hand_out,
-        out_shape=tuple(jax.ShapeDtypeStruct(a.shape, a.dtype) for a in results),
-        in_specs=[vmem] * 3,
-        out_specs=(vmem,) * 3,
-    )(*results)
     return loss, jnp.swapaxes(dx, 0, 1)[None], dw.reshape(1, 14, E)
 
 

time: 104 us -> 103 us (level)
  Pallas kernels: 102 us -> 99.1 us
  local copies, waits for them, and re-layouts: 0 us -> 1.97 us
    pallas_call x2 -> x1, Pallas kernels: 102 us -> 99.1 us  [local(): pl.pallas_call(kernel, out_shape=(pltpu.VMEM((1, 512), F32), pltpu.VMEM((...]
    unnamed x0 -> x3, local copies, waits for them, and re-layouts: none -> 1.97 us
where the time goes in v5:
time: 103 us; the launch traced here: 102 us
  Pallas kernels  99.1 us (96%)
  local copies, waits for them, and re-layouts  1.97 us (2%)
    pallas_call x1, Pallas kernels, local(): pl.pallas_call(kernel, out_shape=(pltpu.VMEM((1, 512), F32), pltpu.VMEM((...  99.1 us

profile of v5, /device:TPU:6, one launch (start us, length us, event | category | flops | bytes accessed | tf_op | source)
XLA Modules:
  0.0 101.8 jit_solution(3970133447374098103)
XLA Ops:
  0.6 99.1 %shard_map.58 = (f32[1,512]{1,0:T(1,128)S(1)}, bf16[448,512]{1,0:T(8,128)(2,1)S(1)}, f32[14,1,1152]{2,1,0:T(1,128)S(1)}) custom-call(bf16[448,512]{1,0:T(8,128)(2,1)} %bitcast.12, bf16[448,1152]{1,0:T(8,128)(2,1)} %bitcast.11, s32[4,128]{1,0:T(4,128)} %bitcast.13), custom_call_target="tpu_custom_call" | custom-call | flops 11000000512 | bytes 2000000 | tf_op jit(solution)/shard_map/pallas_call | solution.py:551
  99.8 0.6 copy.9
  100.4 0.8 copy.10
  101.1 0.6 copy.11

commit v6 on v5

--- a/solution.py
+++ b/solution.py
@@ -56,7 +56,7 @@
     }
     z_dev = (far[1, 0], far[7, 0])
     x_far = far[0, 1]
-    others = (x_same, x_other, *y_dev, sibling, *far.values())
+    others = (x_same, x_other, *y_dev, sibling, *z_dev, x_far)
 
     def send(src, dst, ss, rs, dev):
         pltpu.make_async_remote_copy(

time: 103 us -> 101 us (0.981)
  Pallas kernels: 99.1 us -> 96.7 us
    pallas_call x1, Pallas kernels: 99.1 us -> 96.7 us  [local(): pl.pallas_call(kernel, out_shape=(pltpu.VMEM((1, 512), F32), pltpu.VMEM((...]
where the time goes in v6:
time: 101 us; the launch traced here: 99.3 us
  Pallas kernels  96.7 us (96%)
  local copies, waits for them, and re-layouts  1.97 us (2%)
    pallas_call x1, Pallas kernels, local(): pl.pallas_call(kernel, out_shape=(pltpu.VMEM((1, 512), F32), pltpu.VMEM((...  96.7 us

profile of v6, /device:TPU:6, one launch (start us, length us, event | category | flops | bytes accessed | tf_op | source)
XLA Modules:
  0.0 99.3 jit_solution(7186520249378060249)
XLA Ops:
  0.6 96.7 %shard_map.58 = (f32[1,512]{1,0:T(1,128)S(1)}, bf16[448,512]{1,0:T(8,128)(2,1)S(1)}, f32[14,1,1152]{2,1,0:T(1,128)S(1)}) custom-call(bf16[448,512]{1,0:T(8,128)(2,1)} %bitcast.12, bf16[448,1152]{1,0:T(8,128)(2,1)} %bitcast.11, s32[4,128]{1,0:T(4,128)} %bitcast.13), custom_call_target="tpu_custom_call" | custom-call | flops 11000000512 | bytes 2000000 | tf_op jit(solution)/shard_map/pallas_call | solution.py:551
  97.4 0.6 copy.9
  97.9 0.8 copy.10
  98.7 0.6 copy.11
